TPU v7x, 32 devices: a whole 2x2x4 slice. The times are simulated.
32 devices in a mesh: seq: 8 (over z, y), grp: 4 (over x, core).
Axes of the slice: x: 2, y: 2, z: 4, core: 2. Of those that a mesh axis runs over, the one named last changes fastest.
Arguments:
- queries: bfloat16 [4, 4096, 2048], P('grp', 'seq'), may hold values from -12 to 12
- keys: bfloat16 [4, 4096, 2048], P('grp', 'seq'), may hold values from -4 to 4
- values: bfloat16 [4, 4096, 2048], P('grp', 'seq'), may hold values from -6 to 6
- grad_out: bfloat16 [4, 4096, 2048], P('grp', 'seq'), may hold values from -6 to 6
- out_weight: bfloat16 [2048, 2048], replicated, may hold values from -0.125 to 0.125
- segments: int32 [4, 4096], P('grp', 'seq'), may hold values from 0 to 31, never falling along the last dimension, each value on 1 to 512 neighbouring positions
Outputs:
- grad_queries: bfloat16 [4, 4096, 2048], P('grp', 'seq')
- grad_keys: bfloat16 [4, 4096, 2048], P('grp', 'seq')
- grad_values: bfloat16 [4, 4096, 2048], P('grp', 'seq')
- grad_weight: bfloat16 [2048, 2048], P('seq')
Inputs may be any that keep to these rules, and one draw needn't show every extreme that they name: `segments`: document numbers never fall along a sequence; every document holds 1 to 512 positions and one holds exactly 512.
All inputs are finite; a program needn't handle non-finite values.
Results may differ from a plain program's by a relative error of at most 0.012.
Values may be sent and summed in bfloat16 or wider, within the bound.
A program may use at most 192 MiB of HBM per device.

v0:
```python
import jax
import jax.numpy as jnp
from jax import lax
from jax.sharding import PartitionSpec as P

HEADS = 16


def from_behind(shard, axis, by):
    length = lax.axis_size(axis)
    pairs = [(i, i + by) for i in range(length) if 0 <= i + by < length]
    return lax.ppermute(shard, axis, pairs)


def alibi_slopes():
    head_ids = jnp.arange(HEADS, dtype=jnp.float32)
    return 2.0 ** (-(17.0 + head_ids) / 4.0)


def local(queries, keys, values, grad_out, out_weight, segments):
    query_rows = queries[0]
    key_rows = keys[0]
    value_rows = values[0]
    grad_rows = grad_out[0]
    seg_local = segments[0]
    tok_rows, full_width = query_rows.shape
    head_dim = full_width // HEADS
    score_scale = head_dim ** (-0.5)
    shard_index = lax.axis_index("seq")
    positions = jnp.arange(tok_rows, dtype=jnp.int32)
    query_pos = shard_index * tok_rows + positions
    slopes = alibi_slopes()
    query_heads = query_rows.reshape(tok_rows, HEADS, head_dim)
    fetched = [(key_rows, value_rows, seg_local)]
    hop_index = 1
    fetched.append(from_behind((key_rows, value_rows, seg_local), "seq", hop_index))

    def tile_mask(hop_index):
        seg_part = fetched[hop_index][2]
        key_pos = (shard_index - hop_index) * tok_rows + positions
        allowed = (
            (seg_local[:, None] == seg_part[None, :])
            & (key_pos[None, :] <= query_pos[:, None])
            & (shard_index >= hop_index)
        )
        return (allowed[None], key_pos)

    def tile_scores(hop_index):
        key_part, value_part, seg_part = fetched[hop_index]
        allowed, key_pos = tile_mask(hop_index)
        distance = (query_pos[:, None] - key_pos[None, :]).astype(jnp.float32)
        key_heads = key_part.reshape(tok_rows, HEADS, head_dim)
        value_heads = value_part.reshape(tok_rows, HEADS, head_dim)
        scores = (
            jnp.einsum("qhd,khd->hqk", query_heads, key_heads, preferred_element_type=jnp.float32)
            * score_scale
        )
        scores = scores - slopes[:, None, None] * distance[None]
        return (scores, allowed, key_heads, value_heads)

    def stat_maker(hop_index):
        scores, allowed, key_heads, value_heads = tile_scores(hop_index)
        top = jnp.max(jnp.where(allowed, scores, -1e30), axis=-1)
        total = jnp.sum(jnp.where(allowed, jnp.exp(scores - top[:, :, None]), 0.0), axis=-1)
        return (scores, top, total)

    first_scores, running_top, running_total = stat_maker(0)
    kept_scores = [first_scores]
    hop_index = 1
    hop_scores, new_top_part, new_total = stat_maker(hop_index)
    kept_scores.append(hop_scores)
    merged_top = jnp.maximum(running_top, new_top_part)
    running_total = running_total * jnp.exp(running_top - merged_top) + new_total * jnp.exp(
        new_top_part - merged_top
    )
    log_total = merged_top + jnp.log(running_total)

    def context_maker(hop_index):
        allowed, key_pos = tile_mask(hop_index)
        value_heads = fetched[hop_index][1].reshape(tok_rows, HEADS, head_dim)
        weights = jnp.where(
            allowed, jnp.exp(kept_scores[hop_index] - log_total[:, :, None]), 0.0
        ).astype(jnp.bfloat16)
        return jnp.einsum("hqk,khd->qhd", weights, value_heads, preferred_element_type=jnp.float32)

    context_sum = context_maker(0)
    hop_index = 1
    context_sum = context_sum + context_maker(hop_index)
    context = context_sum.astype(jnp.bfloat16).reshape(tok_rows, full_width)
    grad_context = lax.dot_general(
        grad_rows, out_weight, (((1,), (1,)), ((), ())), preferred_element_type=jnp.float32
    ).astype(jnp.bfloat16)
    grad_heads = grad_context.reshape(tok_rows, HEADS, head_dim)
    context_heads = context.reshape(tok_rows, HEADS, head_dim)
    delta = jnp.sum(grad_heads.astype(jnp.float32) * context_heads.astype(jnp.float32), axis=-1).T

    def backward_maker(hop_index):
        scores, allowed, key_heads, value_heads = tile_scores(hop_index)
        probs = jnp.where(allowed, jnp.exp(scores - log_total[:, :, None]), 0.0)
        weights = probs.astype(jnp.bfloat16)
        dprob = jnp.einsum(
            "qhd,khd->hqk", grad_heads, value_heads, preferred_element_type=jnp.float32
        )
        dscore = (probs * (dprob - delta[:, :, None])).astype(jnp.bfloat16)
        grad_q = jnp.einsum("hqk,khd->qhd", dscore, key_heads, preferred_element_type=jnp.float32)
        grad_k = (
            jnp.einsum("hqk,qhd->khd", dscore, query_heads, preferred_element_type=jnp.float32)
            * score_scale
        )
        grad_v = jnp.einsum("hqk,qhd->khd", weights, grad_heads, preferred_element_type=jnp.float32)
        return (grad_q, grad_k.reshape(tok_rows, full_width), grad_v.reshape(tok_rows, full_width))

    grad_q_sum, first_k, first_v = backward_maker(0)
    parts_k = [first_k]
    parts_v = [first_v]
    hop_index = 1
    grad_q_part, grad_k_part, grad_v_part = backward_maker(hop_index)
    grad_q_sum = grad_q_sum + grad_q_part
    parts_k.append(grad_k_part)
    parts_v.append(grad_v_part)
    total_k = parts_k[0]
    total_v = parts_v[0]
    hop_index = 1
    back_k, back_v = from_behind((parts_k[hop_index], parts_v[hop_index]), "seq", -hop_index)
    total_k = total_k + back_k
    total_v = total_v + back_v
    grad_query = (grad_q_sum * score_scale).astype(jnp.bfloat16).reshape(tok_rows, full_width)
    grad_key = total_k.astype(jnp.bfloat16)
    grad_value = total_v.astype(jnp.bfloat16)
    seq_rows = lax.psum_scatter(
        lax.dot_general(
            context, grad_rows, (((0,), (0,)), ((), ())), preferred_element_type=jnp.float32
        ),
        "seq",
        scatter_dimension=0,
        tiled=True,
    )
    grad_weight = lax.psum(seq_rows, "grp").astype(jnp.bfloat16)
    return (grad_query[None], grad_key[None], grad_value[None], grad_weight)


def solution(mesh):
    placed = (
        P("grp", "seq", None),
        P("grp", "seq", None),
        P("grp", "seq", None),
        P("grp", "seq", None),
        P(),
        P("grp", "seq"),
    )
    return jax.shard_map(
        local,
        mesh=mesh,
        in_specs=placed,
        out_specs=(
            P("grp", "seq", None),
            P("grp", "seq", None),
            P("grp", "seq", None),
            P("seq", None),
        ),
        check_vma=False,
    )
```

profile of v0, /device:TPU:0, one launch (start us, length us, event | category | flops | bytes accessed | tf_op | source)
XLA Modules:
  0.0 643.5 jit_solution(9001799702389281061)
XLA Ops:
  7.2 0.0 copy-start
  7.2 0.0 reduce-scatter.2.cloned.1.call-start
  7.2 5.0 collective-permute-start
  12.2 3.9 copy.85
  16.2 4.7 collective-permute-start.1
  20.9 3.5 collective-permute-start.2
  24.4 1.5 subtract_convert_fusion
  25.9 0.0 copy-done
  25.9 9.1 %convolution_convert_fusion = bf16[512,2048]{1,0:T(8,128)(2,1)} fusion(bf16[2048,2048]{1,0:T(8,128)(2,1)} %param.10, bf16[1,512,2048]{2,1,0:T(8,128)(2,1)S(1)} %copy-done), kind=kOutput, calls=%fused_computation.17 | convolution fusion | flops 4296015872 | bytes 12582912 | tf_op jit(solution)/shard_map/dot_general | solution.py:90
  35.0 3.9 copy.88
  39.0 3.9 copy.86
  42.9 3.9 copy.87
  46.8 0.0 collective-permute-done
  46.8 0.0 copy-done.14
  46.8 1.4 and_and_fusion.1
  48.2 7.1 %select_reduce_fusion.3 = (f32[16,512]{1,0:T(8,128)S(1)}, f32[16,512,512]{1,2,0:T(8,128)S(1)}) fusion(pred[512,512]{0,1:T(8,128)(4,1)} %get-tuple-element.12, f32[512,512]{0,1:T(8,128)} %get-tuple-element.15, f32[16]{0:T(128)S(1)} %multiply_power_fusion, bf16[512,16,128]{0,2,1:T(8,128)(2,1)} %bitcast.69, bf16[512,16,128]{0,2,1:T(8,128)(2,1)} %bitcast.78), kind=kOutput, calls=%fused_computation.8 | convolution fusion | flops 1094705152 | bytes 22315072 | tf_op jit(solution)/shard_map/qhd,khd->hqk/dot_general | solution.py:55
  55.4 0.0 copy-start.12
  55.4 0.0 copy-start.2
  55.4 10.6 %collective-permute-done.1 = bf16[512,2048]{0,1:T(8,128)(2,1)} collective-permute-done((bf16[512,2048]{0,1:T(8,128)(2,1)}, bf16[512,2048]{0,1:T(8,128)(2,1)}, u32[]{:S(2)}, u32[]{:S(2)}) %collective-permute-start.1) | collective-permute-done | bytes 2097184 | tf_op jit(solution)/shard_map/ppermute | solution.py:12
  66.0 0.0 copy-done.7
  66.0 10.8 %select_reduce_fusion.2 = (f32[16,512]{1,0:T(8,128)}, f32[16,512,512]{1,2,0:T(8,128)}) fusion(pred[512,512]{0,1:T(8,128)(4,1)} %get-tuple-element.13, f32[512,512]{0,1:T(8,128)} %get-tuple-element.14, f32[16]{0:T(128)S(1)} %multiply_power_fusion, bf16[512,16,128]{0,2,1:T(8,128)(2,1)S(1)} %bitcast.72, bf16[512,16,128]{0,2,1:T(8,128)(2,1)} %bitcast.2), kind=kOutput, calls=%fused_computation.6 | convolution fusion | flops 1094705152 | bytes 22315072 | tf_op jit(solution)/shard_map/qhd,khd->hqk/dot_general | solution.py:55
  76.8 0.0 copy-done.12
  76.8 9.4 %select_reduce_fusion = (f32[16,512]{1,0:T(8,128)S(1)}, f32[16,512]{1,0:T(8,128)S(1)}) fusion(f32[16,512,512]{1,2,0:T(8,128)} %get-tuple-element.17, f32[16,512]{1,0:T(8,128)} %get-tuple-element.16, pred[512,512]{0,1:T(8,128)(4,1)} %get-tuple-element.13, f32[16,512,512]{1,2,0:T(8,128)S(1)} %get-tuple-element.19, f32[16,512]{1,0:T(8,128)S(1)} %get-tuple-element.18, ...), kind=kLoop, calls=%fused_computation.4 | loop fusion | flops 25149440 | bytes 34209792 | tf_op jit(solution)/shard_map/reduce_sum | solution.py:64
  86.2 0.0 copy-done.13
  86.2 0.8 log_add_fusion
  87.0 0.0 copy-done.2
  87.0 0.0 copy-done.6
  87.0 5.5 fusion.12
  92.6 16.8 %collective-permute-done.2 = bf16[512,2048]{1,0:T(8,128)(2,1)} collective-permute-done((bf16[512,2048]{1,0:T(8,128)(2,1)}, bf16[512,2048]{1,0:T(8,128)(2,1)}, u32[]{:S(2)}, u32[]{:S(2)}) %collective-permute-start.2) | collective-permute-done | bytes 2097184 | tf_op jit(solution)/shard_map/ppermute | solution.py:12
  109.4 4.1 copy.51
  113.6 0.0 copy-done.11
  113.6 11.8 %multiply_reduce_fusion = (f32[512,16]{0,1:T(8,128)S(1)}, bf16[16,512,128]{1,2,0:T(8,128)(2,1)S(1)}) fusion(bf16[512,2048]{0,1:T(8,128)(2,1)} %copy.87, f32[16,512,128]{1,2,0:T(8,128)} %fusion.12, bf16[512,16,128]{0,2,1:T(8,128)(2,1)} %bitcast.67, f32[16,512,512]{1,2,0:T(8,128)} %get-tuple-element.17, f32[16,512]{1,0:T(8,128)S(1)} %log_add_fusion, ...), kind=kOutput, calls=%fused_computation.15 | convolution fusion | flops 1092608000 | bytes 27590656 | tf_op jit(solution)/shard_map/hqk,khd->qhd/dot_general | solution.py:84
  125.4 8.2 %fusion.4 = f32[2048,2048]{1,0:T(8,128)} fusion(bf16[512,2048]{0,1:T(8,128)(2,1)S(1)} %bitcast.82, bf16[1,512,2048]{2,1,0:T(8,128)(2,1)S(1)} %copy-done), kind=kOutput, calls=%fused_computation.22 | convolution fusion | flops 4294967296 | bytes 20971520 | tf_op jit(solution)/shard_map/dot_general | solution.py:131
  133.6 0.0 reduce-scatter.2.cloned.1.call-update
  133.6 1.6 copy-done.4
  135.1 10.8 %fusion.7 = f32[16,128,512]{2,1,0:T(8,128)} fusion(bf16[512,16,128]{0,2,1:T(8,128)(2,1)S(1)} %bitcast.61, f32[16,512,512]{1,2,0:T(8,128)} %get-tuple-element.17, f32[16,512]{1,0:T(8,128)S(1)} %log_add_fusion, pred[512,512]{0,1:T(8,128)(4,1)S(1)} %copy-done.11), kind=kOutput, calls=%fused_computation.25 | convolution fusion | flops 1086324736 | bytes 23363584 | tf_op jit(solution)/shard_map/hqk,qhd->khd/dot_general | solution.py:110
  145.9 5.5 copy.70
  151.4 1.3 collective-permute-start.4
  152.7 0.0 copy-done.10
  152.7 10.9 %fusion.10 = f32[16,128,512]{2,1,0:T(8,128)} fusion(bf16[512,16,128]{0,2,1:T(8,128)(2,1)S(1)} %bitcast.62, f32[16,512,512]{1,2,0:T(8,128)} %copy-done.2, f32[16,512]{1,0:T(8,128)S(1)} %log_add_fusion, pred[512,512]{0,1:T(8,128)(4,1)S(1)} %copy-done.10), kind=kOutput, calls=%fused_computation.26 | convolution fusion | flops 1086324736 | bytes 23363584 | tf_op jit(solution)/shard_map/hqk,qhd->khd/dot_general | solution.py:110
  163.6 15.3 %copy.71 = f32[512,2048]{1,0:T(8,128)} copy(f32[512,2048]{0,1:T(8,128)} %bitcast.76) | data formatting | bytes 8388608 | tf_op jit(solution)/shard_map/reshape | solution.py:111
  178.9 9.2 %multiply_convert_fusion = bf16[16,512,512]{1,2,0:T(8,128)(2,1)S(1)} fusion(f32[16,512,512]{1,2,0:T(8,128)} %get-tuple-element.17, bf16[512,16,128]{0,2,1:T(8,128)(2,1)S(1)} %bitcast.63, bf16[512,16,128]{0,2,1:T(8,128)(2,1)} %bitcast.68, f32[16,512]{1,0:T(8,128)S(1)} %bitcast.83, f32[16,512]{1,0:T(8,128)S(1)} %log_add_fusion, pred[512,512]{0,1:T(8,128)(4,1)S(1)} %copy-done.11), kind=kOutput, calls=%fused_computation | convolution fusion | flops 1094713344 | bytes 29687808 | tf_op jit(solution)/shard_map/qhd,khd->hqk/dot_general | solution.py:101
  188.1 0.0 copy-start.5
  188.1 7.9 %convolution_multiply_fusion = f32[16,512,128]{1,2,0:T(8,128)} fusion(bf16[16,512,512]{1,2,0:T(8,128)(2,1)S(1)} %multiply_convert_fusion, bf16[512,16,128]{0,2,1:T(8,128)(2,1)} %bitcast.70), kind=kOutput, calls=%fused_computation.18 | convolution fusion | flops 1074790400 | bytes 14680064 | tf_op jit(solution)/shard_map/hqk,qhd->khd/dot_general | solution.py:107
  196.1 0.0 copy-done.5
  196.1 5.5 copy.64
  201.5 1.3 collective-permute-start.3
  202.8 9.3 %multiply_convert_fusion.1 = bf16[16,512,512]{1,2,0:T(8,128)(2,1)S(1)} fusion(f32[16,512,512]{1,2,0:T(8,128)} %copy-done.2, bf16[512,16,128]{0,2,1:T(8,128)(2,1)S(1)} %bitcast.64, bf16[512,16,128]{0,2,1:T(8,128)(2,1)} %bitcast.65, f32[16,512]{1,0:T(8,128)S(1)} %bitcast.84, f32[16,512]{1,0:T(8,128)S(1)} %log_add_fusion, pred[512,512]{0,1:T(8,128)(4,1)S(1)} %copy-done.10), kind=kOutput, calls=%fused_computation.1 | convolution fusion | flops 1094713344 | bytes 29687808 | tf_op jit(solution)/shard_map/qhd,khd->hqk/dot_general | solution.py:101
  212.1 0.0 copy-start.3
  212.1 8.0 %convolution_multiply_fusion.1 = f32[16,512,128]{1,2,0:T(8,128)} fusion(bf16[16,512,512]{1,2,0:T(8,128)(2,1)S(1)} %multiply_convert_fusion.1, bf16[512,16,128]{0,2,1:T(8,128)(2,1)} %bitcast.71), kind=kOutput, calls=%fused_computation.19 | convolution fusion | flops 1074790400 | bytes 14680064 | tf_op jit(solution)/shard_map/hqk,qhd->khd/dot_general | solution.py:107
  220.0 0.0 copy-done.3
  220.0 5.6 copy.65
  225.7 0.0 copy-done.9
  225.7 4.7 fusion.20
  230.3 5.5 multiply_convert_fusion.2
  235.8 2.4 copy.72
  238.2 31.8 %collective-permute-done.4 = f32[512,2048]{1,0:T(8,128)} collective-permute-done((f32[512,2048]{1,0:T(8,128)}, f32[512,2048]{1,0:T(8,128)}, u32[]{:S(2)}, u32[]{:S(2)}) %collective-permute-start.4) | collective-permute-done | bytes 4194336 | tf_op jit(solution)/shard_map/ppermute | solution.py:12
  270.1 5.5 fusion.3
  275.5 105.6 %collective-permute-done.3 = f32[512,2048]{1,0:T(8,128)} collective-permute-done((f32[512,2048]{1,0:T(8,128)}, f32[512,2048]{1,0:T(8,128)}, u32[]{:S(2)}, u32[]{:S(2)}) %collective-permute-start.3) | collective-permute-done | bytes 4194336 | tf_op jit(solution)/shard_map/ppermute | solution.py:12
  381.1 0.0 copy-done.8
  381.1 4.3 fusion.2
  385.4 208.6 %reduce-scatter.2.cloned.1.call-done = f32[256,2048]{1,0:T(8,128)} async-done(((f32[2048,2048]{1,0:T(8,128)}), f32[256,2048]{1,0:T(8,128)}) %reduce-scatter.2.cloned.1.call-update) | async-done | bytes 2097168 | tf_op jit(solution)/shard_map/reduce_scatter | solution.py:130
  594.0 42.5 %all-reduce.1 = bf16[256,2048]{1,0:T(8,128)(2,1)} all-reduce(f32[256,2048]{1,0:T(8,128)} %reduce-scatter.2.cloned.1.call-done), channel_id=1, replica_groups=mesh['seq'=8,'grp'=4] {'grp'}, use_global_device_ids=true, to_apply=%region_6.7 | all-reduce | flops 524288 | bytes 3145728 | tf_op jit(solution)/shard_map/psum | solution.py:138
  636.5 0.0 copy-done.1
  (13 shorter events, 0.0 us)
Async XLA Ops:
  7.2 18.8 %copy-start = (bf16[1,512,2048]{2,1,0:T(8,128)(2,1)S(1)}, bf16[1,512,2048]{2,1,0:T(8,128)(2,1)}, u32[]{:S(2)}) copy-start(bf16[1,512,2048]{2,1,0:T(8,128)(2,1)} %param.9) | copy-start | bytes 6291460
  7.2 586.8 %reduce-scatter.2.cloned.1.call-start = ((), (), s32[]{:S(2)}) async-start(), calls=%async_computation.1 | async-start | bytes 18874368 | tf_op jit(solution)/shard_map/reduce_scatter | solution.py:130
  7.2 39.6 %collective-permute-start = (s32[512]{0:T(512)}, s32[512]{0:T(512)S(1)}, u32[]{:S(2)}, u32[]{:S(2)}) collective-permute-start(s32[512]{0:T(512)} %bitcast.85), channel_id=1, source_target_pairs={{0,4},{4,8},{8,12},{12,16},{16,20},{20,24},{24,28},{1,5},{5,9},{9,... | collective-permute-start | bytes 6152 | tf_op jit(solution)/shard_map/ppermute | solution.py:12
  16.2 49.8 %collective-permute-start.1 = (bf16[512,2048]{0,1:T(8,128)(2,1)}, bf16[512,2048]{0,1:T(8,128)(2,1)}, u32[]{:S(2)}, u32[]{:S(2)}) collective-permute-start(bf16[512,2048]{0,1:T(8,128)(2,1)} %bitcast.77), channel_id=1, source_target_pairs={{0,4},{4,8},{8,12},{12,16},{16,20},{20,24},{24,28},{1,5},{5,9},{9,... | collective-permute-start | bytes 6291464 | tf_op jit(solution)/shard_map/ppermute | solution.py:12
  20.9 88.5 %collective-permute-start.2 = (bf16[512,2048]{1,0:T(8,128)(2,1)}, bf16[512,2048]{1,0:T(8,128)(2,1)}, u32[]{:S(2)}, u32[]{:S(2)}) collective-permute-start(bf16[512,2048]{1,0:T(8,128)(2,1)} %bitcast.81), channel_id=1, source_target_pairs={{0,4},{4,8},{8,12},{12,16},{16,20},{20,24},{24,28},{1,5},{5,9},{9,... | collective-permute-start | bytes 6291464 | tf_op jit(solution)/shard_map/ppermute | solution.py:12
  39.0 7.9 %copy-start.14 = (s32[1,512]{1,0:T(1,128)S(1)}, s32[1,512]{1,0:T(1,128)}, u32[]{:S(2)}) copy-start(s32[1,512]{1,0:T(1,128)} %param.11) | copy-start | bytes 6148
  48.2 17.7 %copy-start.7 = (bf16[1,512,2048]{1,2,0:T(8,128)(2,1)S(1)}, bf16[1,512,2048]{1,2,0:T(8,128)(2,1)}, u32[]{:S(2)}) copy-start(bf16[1,512,2048]{1,2,0:T(8,128)(2,1)} %copy.86) | copy-start | bytes 6291460
  55.4 21.4 %copy-start.12 = (f32[16,512]{1,0:T(8,128)}, f32[16,512]{1,0:T(8,128)S(1)}, u32[]{:S(2)}) copy-start(f32[16,512]{1,0:T(8,128)S(1)} %get-tuple-element.18) | copy-start | bytes 98308
  55.4 31.6 %copy-start.2 = (f32[16,512,512]{1,2,0:T(8,128)}, f32[16,512,512]{1,2,0:T(8,128)S(1)}, u32[]{:S(2)}) copy-start(f32[16,512,512]{1,2,0:T(8,128)S(1)} %get-tuple-element.19) | copy-start | bytes 50331652
  76.8 9.4 %copy-start.13 = (f32[16,512]{1,0:T(8,128)S(1)}, f32[16,512]{1,0:T(8,128)}, u32[]{:S(2)}) copy-start(f32[16,512]{1,0:T(8,128)} %get-tuple-element.16) | copy-start | bytes 98308
  76.8 10.2 %copy-start.6 = (bf16[1,512,2048]{1,2,0:T(8,128)(2,1)S(1)}, bf16[1,512,2048]{1,2,0:T(8,128)(2,1)}, u32[]{:S(2)}) copy-start(bf16[1,512,2048]{1,2,0:T(8,128)(2,1)} %copy.88) | copy-start | bytes 6291460
  92.6 21.0 %copy-start.11 = (pred[512,512]{0,1:T(8,128)(4,1)S(1)}, pred[512,512]{0,1:T(8,128)(4,1)}, u32[]{:S(2)}) copy-start(pred[512,512]{0,1:T(8,128)(4,1)} %get-tuple-element.13) | copy-start | bytes 786436
  133.5 1.6 copy-start.4
  145.9 6.8 %copy-start.10 = (pred[512,512]{0,1:T(8,128)(4,1)S(1)}, pred[512,512]{0,1:T(8,128)(4,1)}, u32[]{:S(2)}) copy-start(pred[512,512]{0,1:T(8,128)(4,1)} %get-tuple-element.12) | copy-start | bytes 786436
  151.4 118.6 %collective-permute-start.4 = (f32[512,2048]{1,0:T(8,128)}, f32[512,2048]{1,0:T(8,128)}, u32[]{:S(2)}, u32[]{:S(2)}) collective-permute-start(f32[512,2048]{1,0:T(8,128)} %copy.70), channel_id=1, source_target_pairs={{4,0},{8,4},{12,8},{16,12},{20,16},{24,20},{28,24},{5,1},{9,5},{13... | collective-permute-start | bytes 12582920 | tf_op jit(solution)/shard_map/ppermute | solution.py:12
  188.1 7.9 %copy-start.5 = (bf16[16,512,512]{1,2,0:T(8,128)(2,1)}, bf16[16,512,512]{1,2,0:T(8,128)(2,1)S(1)}, u32[]{:S(2)}) copy-start(bf16[16,512,512]{1,2,0:T(8,128)(2,1)S(1)} %multiply_convert_fusion) | copy-start | bytes 25165828
  201.5 179.6 %collective-permute-start.3 = (f32[512,2048]{1,0:T(8,128)}, f32[512,2048]{1,0:T(8,128)}, u32[]{:S(2)}, u32[]{:S(2)}) collective-permute-start(f32[512,2048]{1,0:T(8,128)} %copy.64), channel_id=1, source_target_pairs={{4,0},{8,4},{12,8},{16,12},{20,16},{24,20},{28,24},{5,1},{9,5},{13... | collective-permute-start | bytes 12582920 | tf_op jit(solution)/shard_map/ppermute | solution.py:12
  212.1 8.0 %copy-start.3 = (bf16[16,512,512]{1,2,0:T(8,128)(2,1)}, bf16[16,512,512]{1,2,0:T(8,128)(2,1)S(1)}, u32[]{:S(2)}) copy-start(bf16[16,512,512]{1,2,0:T(8,128)(2,1)S(1)} %multiply_convert_fusion.1) | copy-start | bytes 25165828
  220.0 5.6 copy-start.9
  238.2 142.9 %copy-start.8 = (f32[512,2048]{1,0:T(8,128)S(1)}, f32[512,2048]{1,0:T(8,128)}, u32[]{:S(2)}) copy-start(f32[512,2048]{1,0:T(8,128)} %copy.65) | copy-start | bytes 12582916
  381.1 255.4 %copy-start.1 = (bf16[1,512,2048]{2,1,0:T(8,128)(2,1)S(1)}, bf16[1,512,2048]{2,1,0:T(8,128)(2,1)}, u32[]{:S(2)}) copy-start(bf16[1,512,2048]{2,1,0:T(8,128)(2,1)} %param.9) | copy-start | bytes 6291460
Sparse Core Ops, SparseCore 0:
  133.7 460.2 reduce-scatter.1
where the time goes:
time: 653 us; the launch traced here: 644 us
  waiting for transfers between devices  373 us (57%)
  matrix products  119 us (18%)
  local copies, waits for them, and re-layouts  55.7 us (9%)
  blocking collectives  42.5 us (7%)
  other arithmetic  22.9 us (4%)
  starting transfers between devices  15.8 us (2%)
  between operations  14.4 us (2%)
    reduce_scatter x1, waiting for transfers between devices, local(): lax.psum_scatter(lax.dot_general(context, grad_rows, (((0,), (0,)), ((),...  209 us
    ppermute x5, waiting for transfers between devices, from_behind(): return lax.ppermute(shard, axis, pairs)  165 us
    psum x1, blocking collectives, local(): grad_weight = lax.psum(seq_rows, 'grp').astype(jnp.bfloat16)  42.5 us
    dot_general x2, matrix products, backward_maker(): jnp.einsum('hqk,qhd->khd', weights, grad_heads, preferred_element_type=jn...  21.6 us
    reshape x2, local copies, waits for them, and re-layouts, backward_maker(): grad_v.reshape(tok_rows, full_width)  20.8 us
    dot_general x2, matrix products, backward_maker(): jnp.einsum('qhd,khd->hqk', grad_heads, value_heads, preferred_element_typ...  18.5 us
    dot_general x2, matrix products, tile_scores(): jnp.einsum('qhd,khd->hqk', query_heads, key_heads, preferred_element_type...  18 us
    dot_general x2, matrix products, context_maker(): jnp.einsum('hqk,khd->qhd', weights, value_heads, preferred_element_type=j...  17.3 us
  transfers between devices with their start and end apart: 6, of which 5 were waited for; matrix products, arithmetic and copies ran while one was open for 27% of the time, Pallas kernels for 0%

commit v1 on v0

v1 whole, which is shorter than its diff:
```python
import functools

import jax
import jax.numpy as jnp
from jax import lax
from jax.experimental import pallas as pl
from jax.experimental.pallas import tpu as pltpu
from jax.sharding import PartitionSpec as P

HEADS = 16
CHUNKS = 4
WEIGHT_PARTS = 2
LOW = -1e30
PARAMS = dict(vmem_limit_bytes=40 * 1024 * 1024)


def from_behind(shard, axis, by):
    length = lax.axis_size(axis)
    pairs = [(i, i + by) for i in range(length) if 0 <= i + by < length]
    return lax.ppermute(shard, axis, pairs)


def alibi_slopes():
    head_ids = jnp.arange(HEADS, dtype=jnp.float32)
    return 2.0 ** (-(17.0 + head_ids) / 4.0)


def dot_nt(a, b):
    return lax.dot_general(a, b, (((1,), (1,)), ((), ())), preferred_element_type=jnp.float32)


def dot_nn(a, b):
    return lax.dot_general(a, b, (((1,), (0,)), ((), ())), preferred_element_type=jnp.float32)


def dot_tn(a, b):
    return lax.dot_general(a, b, (((0,), (0,)), ((), ())), preferred_element_type=jnp.float32)


def tile_scores(query, key, slope, scale, first_col):
    columns = key.shape[0]
    places = lax.broadcasted_iota(jnp.int32, (1, columns), 1) + first_col
    return dot_nt(query, key) * scale + slope * places.astype(jnp.float32)


def own_mask(seg_col, seg_row):
    rows, columns = seg_col.shape[0], seg_row.shape[1]
    row = lax.broadcasted_iota(jnp.int32, (rows, columns), 0)
    column = lax.broadcasted_iota(jnp.int32, (rows, columns), 1)
    return (seg_col == seg_row) & (column <= row)


def own_forward(scale, slopes, seg_col, seg_row, q, k, v, out, stat):
    rows = q.shape[0]
    slope = slopes[pl.program_id(0)]
    scores = tile_scores(q[...], k[...], slope, scale, rows)
    scores = jnp.where(own_mask(seg_col[...], seg_row[...]), scores, LOW)
    top = jnp.max(scores, axis=1, keepdims=True)
    probs = jnp.exp(scores - top)
    total = jnp.sum(probs, axis=1, keepdims=True)
    mixed = dot_nn(probs.astype(jnp.bfloat16), v[...])
    out[...] = mixed / total
    stat[...] = jnp.broadcast_to(top + jnp.log(total), stat.shape)


def hop_step(scale, base, slopes, seg_col, seg_row, q, kv, grad, out, stat, context, lse, delta, grad_q, grad_kv):
    slope = slopes[pl.program_id(0) + base]
    query, key, value, grad_rows = q[...], kv[0], kv[1], grad[...]
    scores = tile_scores(query, key, slope, scale, 0)
    scores = jnp.where(seg_col[...] == seg_row[...], scores, LOW)
    own = stat[:, 0:1]
    top = jnp.maximum(jnp.max(scores, axis=1, keepdims=True), own)
    raw = jnp.exp(scores - top)
    own_part = jnp.exp(own - top)
    total = own_part + jnp.sum(raw, axis=1, keepdims=True)
    share = 1.0 / total
    probs = raw * share
    weights = probs.astype(jnp.bfloat16)
    mixed = out[...] * (own_part * share) + dot_nn(weights, value)
    rounded = mixed.astype(jnp.bfloat16)
    context[...] = rounded
    row_delta = jnp.sum(
        rounded.astype(jnp.float32) * grad_rows.astype(jnp.float32), axis=1, keepdims=True
    )
    lse[...] = jnp.broadcast_to(top + jnp.log(total), lse.shape)
    delta[...] = jnp.broadcast_to(row_delta, delta.shape)
    dscore = (probs * (dot_nt(grad_rows, value) - row_delta)).astype(jnp.bfloat16)
    grad_q[...] = dot_nn(dscore, key)
    grad_kv[0] = (dot_tn(dscore, query) * scale).astype(jnp.bfloat16)
    grad_kv[1] = dot_tn(weights, grad_rows).astype(jnp.bfloat16)


def own_backward(scale, base, slopes, seg_col, seg_row, q, k, v, grad, lse, delta, hop_q, grad_q, grad_kv):
    rows = q.shape[0]
    slope = slopes[pl.program_id(0) + base]
    query, key, value, grad_rows = q[...], k[...], v[...], grad[...]
    scores = tile_scores(query, key, slope, scale, rows)
    scores = jnp.where(own_mask(seg_col[...], seg_row[...]), scores, LOW)
    probs = jnp.exp(scores - lse[:, 0:1])
    weights = probs.astype(jnp.bfloat16)
    dscore = (probs * (dot_nt(grad_rows, value) - delta[:, 0:1])).astype(jnp.bfloat16)
    grad_q[...] = ((dot_nn(dscore, key) + hop_q[...]) * scale).astype(jnp.bfloat16)
    grad_kv[0] = dot_tn(dscore, query) * scale
    grad_kv[1] = dot_tn(weights, grad_rows)


def local(queries, keys, values, grad_out, out_weight, segments):
    query_rows = queries[0]
    key_rows = keys[0]
    value_rows = values[0]
    grad_rows = grad_out[0]
    tok_rows, full_width = query_rows.shape
    head_dim = full_width // HEADS
    scale = head_dim ** (-0.5)
    chunk_heads = HEADS // CHUNKS
    width = chunk_heads * head_dim
    slopes = alibi_slopes()
    seg_col = segments.reshape(tok_rows, 1)
    seg_row = segments
    seg_behind = from_behind(segments, "seq", 1)
    seg_behind = jnp.where(lax.axis_index("seq") > 0, seg_behind, -1)

    arrived = []
    for part in range(CHUNKS):
        columns = slice(part * width, (part + 1) * width)
        both = jnp.stack([key_rows[:, columns], value_rows[:, columns]])
        arrived.append(from_behind(both, "seq", 1))

    slope_spec = pl.BlockSpec(memory_space=pltpu.SMEM)
    col_spec = pl.BlockSpec((tok_rows, 1), lambda h: (0, 0))
    row_spec = pl.BlockSpec((1, tok_rows), lambda h: (0, 0))
    part_spec = pl.BlockSpec((tok_rows, head_dim), lambda h: (0, h))
    pair_spec = pl.BlockSpec((2, tok_rows, head_dim), lambda h: (0, 0, h))

    def head_spec(base):
        return pl.BlockSpec((tok_rows, head_dim), lambda h: (0, base + h))

    def cost(heads, dots):
        pairs = heads * tok_rows * tok_rows
        return pl.CostEstimate(
            flops=2 * dots * pairs * head_dim,
            bytes_accessed=16 * heads * tok_rows * head_dim,
            transcendentals=pairs,
        )

    full = jax.ShapeDtypeStruct((tok_rows, full_width), jnp.float32)
    part_f32 = jax.ShapeDtypeStruct((tok_rows, width), jnp.float32)
    part_bf16 = jax.ShapeDtypeStruct((tok_rows, width), jnp.bfloat16)

    grad_context = lax.dot_general(
        grad_rows, out_weight, (((1,), (1,)), ((), ())), preferred_element_type=jnp.float32
    ).astype(jnp.bfloat16)

    own_out, own_stat = pl.pallas_call(
        functools.partial(own_forward, scale),
        grid=(HEADS,),
        in_specs=[slope_spec, col_spec, row_spec] + [head_spec(0)] * 3,
        out_specs=[head_spec(0)] * 2,
        out_shape=[full, full],
        compiler_params=pltpu.CompilerParams(**PARAMS),
        cost_estimate=cost(HEADS, 2),
        name="own_forward",
    )(slopes, seg_col, seg_row, query_rows, key_rows, value_rows)

    hops, backs, terms, pieces = [], [], [], []
    for part in range(CHUNKS):
        base = part * chunk_heads
        own_spec = head_spec(base)
        hop = pl.pallas_call(
            functools.partial(hop_step, scale, base),
            grid=(chunk_heads,),
            in_specs=[slope_spec, col_spec, row_spec, own_spec, pair_spec, own_spec, own_spec, own_spec],
            out_specs=[part_spec] * 4 + [pair_spec],
            out_shape=[
                part_bf16,
                part_f32,
                part_f32,
                part_f32,
                jax.ShapeDtypeStruct((2, tok_rows, width), jnp.bfloat16),
            ],
            compiler_params=pltpu.CompilerParams(**PARAMS),
            cost_estimate=cost(chunk_heads, 6),
            name="hop_step",
        )(slopes, seg_col, seg_behind, query_rows, arrived[part], grad_context, own_out, own_stat)
        hops.append(hop)
        backs.append(from_behind(hop[4], "seq", -1))
        pieces.append(hop[0])
        if (part + 1) % (CHUNKS // WEIGHT_PARTS) == 0:
            context = jnp.concatenate(pieces, axis=1)
            pieces = []
            term = lax.dot_general(
                context, grad_rows, (((0,), (0,)), ((), ())), preferred_element_type=jnp.float32
            ).astype(jnp.bfloat16)
            terms.append(lax.psum_scatter(term, "grp", scatter_dimension=1, tiled=True))

    weight_term = lax.psum_scatter(
        jnp.concatenate(terms, axis=0), "seq", scatter_dimension=0, tiled=True
    )
    grad_weight = lax.all_gather(weight_term, "grp", axis=1, tiled=True)

    grads_q, grads_k, grads_v = [], [], []
    for part in range(CHUNKS):
        base = part * chunk_heads
        own_spec = head_spec(base)
        _, lse, delta, hop_q, _ = hops[part]
        grad_q, grad_kv = pl.pallas_call(
            functools.partial(own_backward, scale, base),
            grid=(chunk_heads,),
            in_specs=[slope_spec, col_spec, row_spec] + [own_spec] * 4 + [part_spec] * 3,
            out_specs=[part_spec, pair_spec],
            out_shape=[part_bf16, jax.ShapeDtypeStruct((2, tok_rows, width), jnp.float32)],
            compiler_params=pltpu.CompilerParams(**PARAMS),
            cost_estimate=cost(chunk_heads, 5),
            name="own_backward",
        )(slopes, seg_col, seg_row, query_rows, key_rows, value_rows, grad_context, lse, delta, hop_q)
        total = (grad_kv + backs[part].astype(jnp.float32)).astype(jnp.bfloat16)
        grads_q.append(grad_q)
        grads_k.append(total[0])
        grads_v.append(total[1])
    grad_query = jnp.concatenate(grads_q, axis=1)
    grad_key = jnp.concatenate(grads_k, axis=1)
    grad_value = jnp.concatenate(grads_v, axis=1)
    return (grad_query[None], grad_key[None], grad_value[None], grad_weight)


def solution(mesh):
    placed = (
        P("grp", "seq", None),
        P("grp", "seq", None),
        P("grp", "seq", None),
        P("grp", "seq", None),
        P(),
        P("grp", "seq"),
    )
    return jax.shard_map(
        local,
        mesh=mesh,
        in_specs=placed,
        out_specs=(
            P("grp", "seq", None),
            P("grp", "seq", None),
            P("grp", "seq", None),
            P("seq", None),
        ),
        check_vma=False,
    )
```

time: 653 us -> 401 us (0.61); the launches traced: 644 us -> 400 us
  waiting for transfers between devices: 373 us -> 185 us
  matrix products: 119 us -> 14.5 us
  Pallas kernels: 0 us -> 87.5 us
  blocking collectives: 42.5 us -> 0 us
  starting transfers between devices: 15.8 us -> 27 us
    dot_general x12 -> x0, matrix products: 101 us -> none  [the longest x2 21.6 us: backward_maker(): jnp.einsum('hqk,qhd->khd', weights, grad_heads, preferred_element_type=jn...]
    ppermute x5 -> x9, waiting for transfers between devices: 165 us -> 65.5 us  [from_behind(): return lax.ppermute(shard, axis, pairs)]
    reduce_scatter x1 -> x3, waiting for transfers between devices: 209 us -> 110 us  [the longest x1 62.7 us: local(): lax.psum_scatter(jnp.concatenate(terms, axis=0), 'seq', scatter_dimension...]
    pallas_call x0 -> x9, Pallas kernels: none -> 87.5 us  [the longest x4 46.7 us: local(): pl.pallas_call(functools.partial(hop_step, scale, base), grid=(chunk_head...]
    psum x1 -> x0, blocking collectives: 42.5 us -> none  [local(): grad_weight = lax.psum(seq_rows, 'grp').astype(jnp.bfloat16)]
    unnamed x31 -> x107, local copies, waits for them, and re-layouts: 4.01 us -> 45.9 us
    reshape x5 -> x1, local copies, waits for them, and re-layouts: 35.8 us -> 0.14 us  [local(): seg_col = segments.reshape(tok_rows, 1)]
    ppermute x5 -> x9, starting transfers between devices: 15.8 us -> 26.8 us  [from_behind(): return lax.ppermute(shard, axis, pairs)]
  transfers between devices with their start and end apart: 6 -> 13, of which waited for: 5 -> 8; matrix products, arithmetic and copies ran while one was open for 27% -> 8% of each run, Pallas kernels for 0% -> 19%
where the time goes in v1:
time: 401 us; the launch traced here: 400 us
  waiting for transfers between devices  185 us (46%)
  Pallas kernels  87.5 us (22%)
  local copies, waits for them, and re-layouts  52.5 us (13%)
  starting transfers between devices  27 us (7%)
  other arithmetic  18.9 us (5%)
  matrix products  14.5 us (4%)
  between operations  14.2 us (4%)
    ppermute x9, waiting for transfers between devices, from_behind(): return lax.ppermute(shard, axis, pairs)  65.5 us
    reduce_scatter x1, waiting for transfers between devices, local(): lax.psum_scatter(jnp.concatenate(terms, axis=0), 'seq', scatter_dimension...  62.7 us
    reduce_scatter x2, waiting for transfers between devices, local(): terms.append(lax.psum_scatter(term, 'grp', scatter_dimension=1, tiled=True))  47.6 us
    pallas_call x4, Pallas kernels, local(): pl.pallas_call(functools.partial(hop_step, scale, base), grid=(chunk_head...  46.7 us
    unnamed x107, local copies, waits for them, and re-layouts  45.9 us
    ppermute x9, starting transfers between devices, from_behind(): return lax.ppermute(shard, axis, pairs)  26.8 us
    pallas_call x4, Pallas kernels, local(): pl.pallas_call(functools.partial(own_backward, scale, base), grid=(chunk_...  22.8 us
    pallas_call x1, Pallas kernels, local(): pl.pallas_call(functools.partial(own_forward, scale), grid=(HEADS,), in_s...  18 us
  transfers between devices with their start and end apart: 13, of which 8 were waited for; matrix products, arithmetic and copies ran while one was open for 8% of the time, Pallas kernels for 19%

profile of v1, /device:TPU:0, one launch (start us, length us, event | category | flops | bytes accessed | tf_op | source)
XLA Modules:
  0.0 399.8 jit_solution(7112572220320321684)
XLA Ops:
  7.2 5.0 %collective-permute-start = (s32[1,512]{1,0:T(1,128)}, s32[1,512]{1,0:T(1,128)S(1)}, u32[]{:S(2)}, u32[]{:S(2)}) collective-permute-start(s32[1,512]{1,0:T(1,128)} %seg_row.9), channel_id=1, source_target_pairs={{0,4},{4,8},{8,12},{12,16},{16,20},{20,24},{24,28},{1,5},{5,9},{9,... | collective-permute-start | bytes 6152 | tf_op jit(solution)/shard_map/ppermute | solution.py:20
  12.2 3.8 slice_bitcast_fusion.14
  16.1 1.1 pad_maximum_fusion.3
  17.2 4.4 %collective-permute-start.3 = (bf16[2,512,512]{2,1,0:T(8,128)(2,1)}, bf16[2,512,512]{2,1,0:T(8,128)(2,1)}, u32[]{:S(2)}, u32[]{:S(2)}) collective-permute-start(bf16[2,512,512]{2,1,0:T(8,128)(2,1)} %pad_maximum_fusion.3), channel_id=1, source_target_pairs={{0,4},{4,8},{8,12},{12,16},{16,20},{20,24},{24,28},{1,5},{5,9},{9,... | collective-permute-start | bytes 3145736 | tf_op jit(solution)/shard_map/ppermute | solution.py:20
  21.6 1.1 pad_maximum_fusion.4
  22.6 2.6 collective-permute-start.4
  25.3 5.8 %convolution_convert_fusion.2.grad = bf16[512,2048]{1,0:T(8,128)(2,1)} fusion(bf16[2048,2048]{1,0:T(8,128)(2,1)S(1)} %copy-done.52, bf16[1,512,2048]{2,1,0:T(8,128)(2,1)S(1)} %copy-done), kind=kOutput, calls=%fused_computation.2 | convolution fusion | flops 4296015872 | bytes 12582912 | tf_op jit(solution)/shard_map/dot_general | solution.py:150
  31.2 1.6 copy-done.2
  32.8 1.6 copy-done.13
  34.4 1.6 copy-done.15
  36.0 18.0 %own_forward.1 = (f32[512,2048]{1,0:T(8,128)S(1)}, f32[512,2048]{1,0:T(8,128)}) custom-call(f32[16]{0:T(128)S(1)} %multiply_power_fusion.slopes, s32[512,1]{1,0:T(8,128)S(1)} %copy.12.seg_col, s32[1,512]{1,0:T(1,128)S(1)} %copy-done.45, bf16[512,2048]{1,0:T(8,128)(2,1)S(1)} %bitcast.50, bf16[512,2048]{1,0:T(8,128)(2,1)S(1)} %bitcast.60, ...), custom_call_target="tpu_custom_call" | custom-call | flops 2147483648 | bytes 16777216 | tf_op jit(solution)/shard_map/own_forward/pallas_call | solution.py:154
  54.0 2.1 copy-done.10
  56.1 9.4 %collective-permute-done.4.kv = bf16[2,512,512]{2,1,0:T(8,128)(2,1)S(1)} collective-permute-done((bf16[2,512,512]{2,1,0:T(8,128)(2,1)}, bf16[2,512,512]{2,1,0:T(8,128)(2,1)S(1)}, u32[]{:S(2)}, u32[]{:S(2)}) %collective-permute-start.4) | collective-permute-done | bytes 1048608 | tf_op jit(solution)/shard_map/ppermute | solution.py:20
  66.5 1.6 copy-done.3
  68.0 1.6 copy-done.6
  69.6 2.2 copy-done.11
  71.8 1.2 copy-done.42
  73.1 11.8 %hop_step.7 = (bf16[512,512]{1,0:T(8,128)(2,1)S(1)}, f32[512,512]{1,0:T(8,128)S(1)}, f32[512,512]{1,0:T(8,128)S(1)}, f32[512,512]{1,0:T(8,128)S(1)}, bf16[2,512,512]{2,1,0:T(8,128)(2,1)S(1)}) custom-call(f32[16]{0:T(128)S(1)} %multiply_power_fusion.slopes, s32[512,1]{1,0:T(8,128)S(1)} %copy.12.seg_col, s32[1,512]{1,0:T(1,128)S(1)} %broadcast_select_fusion.seg_row, ...), custom_call_target="tpu_custom_call" | custom-call | flops 1610612736 | bytes 4194304 | tf_op jit(solution)/shard_map/hop_step/pallas_call | solution.py:169
  87.8 11.6 %hop_step.6 = (bf16[512,512]{1,0:T(8,128)(2,1)S(1)}, f32[512,512]{1,0:T(8,128)S(1)}, f32[512,512]{1,0:T(8,128)S(1)}, f32[512,512]{1,0:T(8,128)S(1)}, bf16[2,512,512]{2,1,0:T(8,128)(2,1)S(1)}) custom-call(f32[16]{0:T(128)S(1)} %multiply_power_fusion.slopes, s32[512,1]{1,0:T(8,128)S(1)} %copy.12.seg_col, s32[1,512]{1,0:T(1,128)S(1)} %broadcast_select_fusion.seg_row, ...), custom_call_target="tpu_custom_call" | custom-call | flops 1610612736 | bytes 4194304 | tf_op jit(solution)/shard_map/hop_step/pallas_call | solution.py:169
  103.3 4.4 %convolution_convert_fusion = bf16[1024,2048]{1,0:T(8,128)(2,1)} fusion(bf16[1,512,2048]{2,1,0:T(8,128)(2,1)S(1)} %copy-done, bf16[512,512]{1,0:T(8,128)(2,1)S(1)} %get-tuple-element.63, bf16[512,512]{1,0:T(8,128)(2,1)S(1)} %get-tuple-element.62), kind=kOutput, calls=%fused_computation | convolution fusion | flops 2151677952 | bytes 7340032 | tf_op jit(solution)/shard_map/dot_general | solution.py:191
  107.8 1.4 pad_maximum_fusion.2
  109.3 4.5 %collective-permute-start.2 = (bf16[2,512,512]{2,1,0:T(8,128)(2,1)S(1)}, bf16[2,512,512]{2,1,0:T(8,128)(2,1)S(1)}, u32[]{:S(2)}, u32[]{:S(2)}) collective-permute-start(bf16[2,512,512]{2,1,0:T(8,128)(2,1)S(1)} %pad_maximum_fusion.2), channel_id=1, source_target_pairs={{0,4},{4,8},{8,12},{12,16},{16,20},{20,24},{24,28},{1,5},{5,9},{9,... | collective-permute-start | bytes 3145736 | tf_op jit(solution)/shard_map/ppermute | solution.py:20
  113.8 1.3 pad_maximum_fusion.1
  115.1 4.8 %collective-permute-start.1 = (bf16[2,512,512]{2,1,0:T(8,128)(2,1)S(1)}, bf16[2,512,512]{2,1,0:T(8,128)(2,1)S(1)}, u32[]{:S(2)}, u32[]{:S(2)}) collective-permute-start(bf16[2,512,512]{2,1,0:T(8,128)(2,1)S(1)} %pad_maximum_fusion.1), channel_id=1, source_target_pairs={{0,4},{4,8},{8,12},{12,16},{16,20},{20,24},{24,28},{1,5},{5,9},{9,... | collective-permute-start | bytes 3145736 | tf_op jit(solution)/shard_map/ppermute | solution.py:20
  119.8 17.5 %collective-permute-done.2.kv = bf16[2,512,512]{2,1,0:T(8,128)(2,1)S(1)} collective-permute-done((bf16[2,512,512]{2,1,0:T(8,128)(2,1)S(1)}, bf16[2,512,512]{2,1,0:T(8,128)(2,1)S(1)}, u32[]{:S(2)}, u32[]{:S(2)}) %collective-permute-start.2) | collective-permute-done | bytes 1048608 | tf_op jit(solution)/shard_map/ppermute | solution.py:20
  137.3 2.2 copy-done.12
  139.5 11.7 %hop_step.5 = (bf16[512,512]{1,0:T(8,128)(2,1)S(1)}, f32[512,512]{1,0:T(8,128)S(1)}, f32[512,512]{1,0:T(8,128)S(1)}, f32[512,512]{1,0:T(8,128)S(1)}, bf16[2,512,512]{2,1,0:T(8,128)(2,1)S(1)}) custom-call(f32[16]{0:T(128)S(1)} %multiply_power_fusion.slopes, s32[512,1]{1,0:T(8,128)S(1)} %copy.12.seg_col, s32[1,512]{1,0:T(1,128)S(1)} %broadcast_select_fusion.seg_row, ...), custom_call_target="tpu_custom_call" | custom-call | flops 1610612736 | bytes 4194304 | tf_op jit(solution)/shard_map/hop_step/pallas_call | solution.py:169
  152.2 1.0 copy-done.31
  155.2 2.2 collective-permute-done.1.kv
  157.4 11.6 %hop_step.4 = (bf16[512,512]{1,0:T(8,128)(2,1)S(1)}, f32[512,512]{1,0:T(8,128)S(1)}, f32[512,512]{1,0:T(8,128)S(1)}, f32[512,512]{1,0:T(8,128)S(1)}, bf16[2,512,512]{2,1,0:T(8,128)(2,1)S(1)}) custom-call(f32[16]{0:T(128)S(1)} %multiply_power_fusion.slopes, s32[512,1]{1,0:T(8,128)S(1)} %copy.12.seg_col, s32[1,512]{1,0:T(1,128)S(1)} %broadcast_select_fusion.seg_row, ...), custom_call_target="tpu_custom_call" | custom-call | flops 1610612736 | bytes 4194304 | tf_op jit(solution)/shard_map/hop_step/pallas_call | solution.py:169
  170.0 1.0 copy-done.37
  171.0 1.0 copy-done.39
  173.0 4.4 %convolution_convert_fusion.1 = bf16[1024,2048]{1,0:T(8,128)(2,1)} fusion(bf16[1,512,2048]{2,1,0:T(8,128)(2,1)S(1)} %copy-done, bf16[512,512]{1,0:T(8,128)(2,1)S(1)} %get-tuple-element.61, bf16[512,512]{1,0:T(8,128)(2,1)S(1)} %get-tuple-element.60), kind=kOutput, calls=%fused_computation.1 | convolution fusion | flops 2151677952 | bytes 7340032 | tf_op jit(solution)/shard_map/dot_general | solution.py:191
  177.5 47.6 %reduce-scatter.4.cloned.1.call-done = bf16[1024,512]{1,0:T(8,128)(2,1)} async-done(((bf16[1024,2048]{1,0:T(8,128)(2,1)}), bf16[1024,512]{1,0:T(8,128)(2,1)}) %reduce-scatter.4.cloned.1.call-update) | async-done | bytes 1048592 | tf_op jit(solution)/shard_map/reduce_scatter | solution.py:194
  225.1 3.0 pad_maximum_fusion
  228.2 1.4 collective-permute-start.8
  229.6 1.3 collective-permute-start.7
  230.9 1.3 collective-permute-start.6
  232.2 1.5 collective-permute-start.5
  233.7 1.6 copy-done.9
  235.3 1.8 copy-done.14
  237.1 1.6 copy-done.16
  238.7 1.2 copy-done.20
  239.9 1.2 copy-done.22
  241.1 5.7 %own_backward.7 = (bf16[512,512]{1,0:T(8,128)(2,1)S(1)}, f32[2,512,512]{2,1,0:T(8,128)S(1)}) custom-call(f32[16]{0:T(128)S(1)} %multiply_power_fusion.slopes, s32[512,1]{1,0:T(8,128)S(1)} %copy.12.seg_col, s32[1,512]{1,0:T(1,128)S(1)} %copy-done.45, bf16[512,2048]{1,0:T(8,128)(2,1)S(1)} %bitcast.55, bf16[512,2048]{1,0:T(8,128)(2,1)S(1)} %bitcast.61, ...), custom_call_target="tpu_custom_call" | custom-call | flops 1342177280 | bytes 4194304 | tf_op jit(solution)/shard_map/own_backward/pallas_call | solution.py:206
  246.9 5.7 %own_backward.6 = (bf16[512,512]{1,0:T(8,128)(2,1)S(1)}, f32[2,512,512]{2,1,0:T(8,128)S(1)}) custom-call(f32[16]{0:T(128)S(1)} %multiply_power_fusion.slopes, s32[512,1]{1,0:T(8,128)S(1)} %copy.12.seg_col, s32[1,512]{1,0:T(1,128)S(1)} %copy-done.45, bf16[512,2048]{1,0:T(8,128)(2,1)S(1)} %bitcast.56, bf16[512,2048]{1,0:T(8,128)(2,1)S(1)} %bitcast.62, ...), custom_call_target="tpu_custom_call" | custom-call | flops 1342177280 | bytes 4194304 | tf_op jit(solution)/shard_map/own_backward/pallas_call | solution.py:206
  253.4 1.3 copy-done.40
  254.7 5.7 %own_backward.4 = (bf16[512,512]{1,0:T(8,128)(2,1)S(1)}, f32[2,512,512]{2,1,0:T(8,128)S(1)}) custom-call(f32[16]{0:T(128)S(1)} %multiply_power_fusion.slopes, s32[512,1]{1,0:T(8,128)S(1)} %copy.12.seg_col, s32[1,512]{1,0:T(1,128)S(1)} %copy-done.45, bf16[512,2048]{1,0:T(8,128)(2,1)S(1)} %bitcast.57, bf16[512,2048]{1,0:T(8,128)(2,1)S(1)} %bitcast.63, ...), custom_call_target="tpu_custom_call" | custom-call | flops 1342177280 | bytes 4194304 | tf_op jit(solution)/shard_map/own_backward/pallas_call | solution.py:206
  260.3 1.3 copy-done.17
  261.7 5.7 %own_backward.5 = (bf16[512,512]{1,0:T(8,128)(2,1)S(1)}, f32[2,512,512]{2,1,0:T(8,128)S(1)}) custom-call(f32[16]{0:T(128)S(1)} %multiply_power_fusion.slopes, s32[512,1]{1,0:T(8,128)S(1)} %copy.12.seg_col, s32[1,512]{1,0:T(1,128)S(1)} %copy-done.45, bf16[512,2048]{1,0:T(8,128)(2,1)S(1)} %bitcast.58, bf16[512,2048]{1,0:T(8,128)(2,1)S(1)} %bitcast.64, ...), custom_call_target="tpu_custom_call" | custom-call | flops 1342177280 | bytes 4194304 | tf_op jit(solution)/shard_map/own_backward/pallas_call | solution.py:206
  267.4 1.6 maximum_bitcast_fusion
  269.0 1.6 add_convert_fusion
  270.7 16.8 %collective-permute-done.7 = bf16[2,512,512]{2,1,0:T(8,128)(2,1)} collective-permute-done((bf16[2,512,512]{2,1,0:T(8,128)(2,1)}, bf16[2,512,512]{2,1,0:T(8,128)(2,1)}, u32[]{:S(2)}, u32[]{:S(2)}) %collective-permute-start.7) | collective-permute-done | bytes 1048608 | tf_op jit(solution)/shard_map/ppermute | solution.py:20
  287.5 1.6 add_convert_fusion.1
  289.1 1.1 slice_bitcast_fusion
  290.1 19.7 %collective-permute-done.6 = bf16[2,512,512]{2,1,0:T(8,128)(2,1)S(1)} collective-permute-done((bf16[2,512,512]{2,1,0:T(8,128)(2,1)}, bf16[2,512,512]{2,1,0:T(8,128)(2,1)S(1)}, u32[]{:S(2)}, u32[]{:S(2)}) %collective-permute-start.6) | collective-permute-done | bytes 1048608 | tf_op jit(solution)/shard_map/ppermute | solution.py:20
  309.8 1.3 add_convert_fusion.2
  311.2 62.7 %reduce-scatter.8.cloned.1.call-done = bf16[256,512]{1,0:T(8,128)(2,1)} async-done(((bf16[2048,512]{1,0:T(8,128)(2,1)}), bf16[256,512]{1,0:T(8,128)(2,1)}) %reduce-scatter.8.cloned.1.call-update) | async-done | bytes 262160 | tf_op jit(solution)/shard_map/reduce_scatter | solution.py:196
  373.9 1.4 slice_bitcast_fusion.2
  375.8 1.6 add_convert_fusion.3
  378.4 1.6 maximum_bitcast_fusion.2
  380.0 1.6 maximum_bitcast_fusion.1
  381.6 9.3 %all-gather.2.cloned.1.call-done = bf16[256,2048]{1,0:T(8,128)(2,1)} async-done(((bf16[256,512]{1,0:T(8,128)(2,1)}), bf16[256,2048]{1,0:T(8,128)(2,1)}) %all-gather.2.cloned.1.call-update) | async-done | bytes 1048592 | tf_op jit(solution)/shard_map/all_gather | solution.py:199
  390.9 2.3 copy.20
  (105 shorter events, 15.5 us)
Async XLA Ops:
  7.2 18.1 %copy-start = (bf16[1,512,2048]{2,1,0:T(8,128)(2,1)S(1)}, bf16[1,512,2048]{2,1,0:T(8,128)(2,1)}, u32[]{:S(2)}) copy-start(bf16[1,512,2048]{2,1,0:T(8,128)(2,1)} %param.9) | copy-start | bytes 6291460
  7.2 170.3 %reduce-scatter.6.cloned.1.call-start = ((), (), s32[]{:S(2)}) async-start(), calls=%async_computation.4 | async-start | bytes 5242880 | tf_op jit(solution)/shard_map/reduce_scatter | solution.py:194
  7.2 48.9 %collective-permute-start = (s32[1,512]{1,0:T(1,128)}, s32[1,512]{1,0:T(1,128)S(1)}, u32[]{:S(2)}, u32[]{:S(2)}) collective-permute-start(s32[1,512]{1,0:T(1,128)} %seg_row.9), channel_id=1, source_target_pairs={{0,4},{4,8},{8,12},{12,16},{16,20},{20,24},{24,28},{1,5},{5,9},{9,... | collective-permute-start | bytes 6152 | tf_op jit(solution)/shard_map/ppermute | solution.py:20
  12.2 13.0 %copy-start.52 = (bf16[2048,2048]{1,0:T(8,128)(2,1)S(1)}, bf16[2048,2048]{1,0:T(8,128)(2,1)}, u32[]{:S(2)}) copy-start(bf16[2048,2048]{1,0:T(8,128)(2,1)} %param.10) | copy-start | bytes 25165828
  17.2 70.6 %collective-permute-start.3 = (bf16[2,512,512]{2,1,0:T(8,128)(2,1)}, bf16[2,512,512]{2,1,0:T(8,128)(2,1)}, u32[]{:S(2)}, u32[]{:S(2)}) collective-permute-start(bf16[2,512,512]{2,1,0:T(8,128)(2,1)} %pad_maximum_fusion.3), channel_id=1, source_target_pairs={{0,4},{4,8},{8,12},{12,16},{16,20},{20,24},{24,28},{1,5},{5,9},{9,... | collective-permute-start | bytes 3145736 | tf_op jit(solution)/shard_map/ppermute | solution.py:20
  22.6 8.4 %copy-start.45 = (s32[1,512]{1,0:T(1,128)S(1)}, s32[1,512]{1,0:T(1,128)}, u32[]{:S(2)}) copy-start(s32[1,512]{1,0:T(1,128)} %seg_row.9) | copy-start | bytes 6148
  22.6 42.8 %collective-permute-start.4 = (bf16[2,512,512]{2,1,0:T(8,128)(2,1)}, bf16[2,512,512]{2,1,0:T(8,128)(2,1)S(1)}, u32[]{:S(2)}, u32[]{:S(2)}) collective-permute-start(bf16[2,512,512]{2,1,0:T(8,128)(2,1)} %pad_maximum_fusion.4), channel_id=1, source_target_pairs={{0,4},{4,8},{8,12},{12,16},{16,20},{20,24},{24,28},{1,5},{5,9},{9,... | collective-permute-start | bytes 3145736 | tf_op jit(solution)/shard_map/ppermute | solution.py:20
  31.2 1.6 copy-start.2
  32.8 1.6 copy-start.13
  34.4 1.6 copy-start.15
  54.0 2.1 copy-start.10
  65.5 1.0 copy-start.41
  66.5 1.6 copy-start.3
  68.0 1.6 copy-start.6
  69.6 2.2 copy-start.11
  71.8 1.2 copy-start.42
  73.1 14.7 %copy-start.7 = (bf16[512,2048]{1,0:T(8,128)(2,1)S(1)}, bf16[512,2048]{1,0:T(8,128)(2,1)}, u32[]{:S(2)}) copy-start(bf16[512,2048]{1,0:T(8,128)(2,1)} %convolution_convert_fusion.2.grad) | copy-start | bytes 6291460
  84.9 1.0 copy-start.19
  85.8 1.0 copy-start.21
  99.4 1.0 copy-start.23
  100.4 1.0 copy-start.25
  101.4 1.0 copy-start.27
  102.4 1.0 copy-start.47
  107.8 117.3 %reduce-scatter.4.cloned.1.call-start = ((), (), s32[]{:S(2)}) async-start(), calls=%async_computation.3 | async-start | bytes 5242880 | tf_op jit(solution)/shard_map/reduce_scatter | solution.py:194
  107.8 29.5 %copy-start.4 = (bf16[1,512,2048]{2,1,0:T(8,128)(2,1)S(1)}, bf16[1,512,2048]{2,1,0:T(8,128)(2,1)}, u32[]{:S(2)}) copy-start(bf16[1,512,2048]{2,1,0:T(8,128)(2,1)} %param.6) | copy-start | bytes 6291460
  107.8 29.5 %copy-start.8 = (bf16[512,2048]{1,0:T(8,128)(2,1)S(1)}, bf16[512,2048]{1,0:T(8,128)(2,1)}, u32[]{:S(2)}) copy-start(bf16[512,2048]{1,0:T(8,128)(2,1)} %convolution_convert_fusion.2.grad) | copy-start | bytes 6291460
  109.3 28.0 %collective-permute-start.2 = (bf16[2,512,512]{2,1,0:T(8,128)(2,1)S(1)}, bf16[2,512,512]{2,1,0:T(8,128)(2,1)S(1)}, u32[]{:S(2)}, u32[]{:S(2)}) collective-permute-start(bf16[2,512,512]{2,1,0:T(8,128)(2,1)S(1)} %pad_maximum_fusion.2), channel_id=1, source_target_pairs={{0,4},{4,8},{8,12},{12,16},{16,20},{20,24},{24,28},{1,5},{5,9},{9,... | collective-permute-start | bytes 3145736 | tf_op jit(solution)/shard_map/ppermute | solution.py:20
  115.1 42.3 %collective-permute-start.1 = (bf16[2,512,512]{2,1,0:T(8,128)(2,1)S(1)}, bf16[2,512,512]{2,1,0:T(8,128)(2,1)S(1)}, u32[]{:S(2)}, u32[]{:S(2)}) collective-permute-start(bf16[2,512,512]{2,1,0:T(8,128)(2,1)S(1)} %pad_maximum_fusion.1), channel_id=1, source_target_pairs={{0,4},{4,8},{8,12},{12,16},{16,20},{20,24},{24,28},{1,5},{5,9},{9,... | collective-permute-start | bytes 3145736 | tf_op jit(solution)/shard_map/ppermute | solution.py:20
  137.3 2.2 copy-start.12
  151.2 1.0 copy-start.29
  152.2 1.0 copy-start.31
  153.3 1.0 copy-start.33
  154.3 1.0 copy-start.49
  169.0 1.0 copy-start.35
  170.0 1.0 copy-start.37
  171.0 1.0 copy-start.39
  172.0 1.0 copy-start.48
  177.4 196.4 %reduce-scatter.8.cloned.1.call-start = ((), (), s32[]{:S(2)}) async-start(), calls=%async_computation.5 | async-start | bytes 2359296 | tf_op jit(solution)/shard_map/reduce_scatter | solution.py:196
  228.1 5.6 %copy-start.5 = (bf16[1,512,2048]{2,1,0:T(8,128)(2,1)S(1)}, bf16[1,512,2048]{2,1,0:T(8,128)(2,1)}, u32[]{:S(2)}) copy-start(bf16[1,512,2048]{2,1,0:T(8,128)(2,1)} %param.6) | copy-start | bytes 6291460
  228.1 162.8 %all-gather.2.cloned.1.call-start = ((), (), s32[]{:S(2)}) async-start(), calls=%async_computation.6 | async-start | bytes 1310720 | tf_op jit(solution)/shard_map/all_gather | solution.py:199
  228.2 40.9 %collective-permute-start.8 = (bf16[2,512,512]{2,1,0:T(8,128)(2,1)}, bf16[2,512,512]{2,1,0:T(8,128)(2,1)}, u32[]{:S(2)}, u32[]{:S(2)}) collective-permute-start(bf16[2,512,512]{2,1,0:T(8,128)(2,1)} %copy-done.46), channel_id=1, source_target_pairs={{4,0},{8,4},{12,8},{16,12},{20,16},{24,20},{28,24},{5,1},{9,5},{13... | collective-permute-start | bytes 3145736 | tf_op jit(solution)/shard_map/ppermute | solution.py:20
  229.6 57.9 %collective-permute-start.7 = (bf16[2,512,512]{2,1,0:T(8,128)(2,1)}, bf16[2,512,512]{2,1,0:T(8,128)(2,1)}, u32[]{:S(2)}, u32[]{:S(2)}) collective-permute-start(bf16[2,512,512]{2,1,0:T(8,128)(2,1)} %copy-done.47), channel_id=1, source_target_pairs={{4,0},{8,4},{12,8},{16,12},{20,16},{24,20},{28,24},{5,1},{9,5},{13... | collective-permute-start | bytes 3145736 | tf_op jit(solution)/shard_map/ppermute | solution.py:20
  230.9 78.9 %collective-permute-start.6 = (bf16[2,512,512]{2,1,0:T(8,128)(2,1)}, bf16[2,512,512]{2,1,0:T(8,128)(2,1)S(1)}, u32[]{:S(2)}, u32[]{:S(2)}) collective-permute-start(bf16[2,512,512]{2,1,0:T(8,128)(2,1)} %copy-done.49), channel_id=1, source_target_pairs={{4,0},{8,4},{12,8},{16,12},{20,16},{24,20},{28,24},{5,1},{9,5},{13... | collective-permute-start | bytes 3145736 | tf_op jit(solution)/shard_map/ppermute | solution.py:20
  232.2 143.1 %collective-permute-start.5 = (bf16[2,512,512]{2,1,0:T(8,128)(2,1)}, bf16[2,512,512]{2,1,0:T(8,128)(2,1)}, u32[]{:S(2)}, u32[]{:S(2)}) collective-permute-start(bf16[2,512,512]{2,1,0:T(8,128)(2,1)} %copy-done.48), channel_id=1, source_target_pairs={{4,0},{8,4},{12,8},{16,12},{20,16},{24,20},{28,24},{5,1},{9,5},{13... | collective-permute-start | bytes 3145736 | tf_op jit(solution)/shard_map/ppermute | solution.py:20
  233.7 1.6 copy-start.9
  235.3 1.8 copy-start.14
  237.1 1.6 copy-start.16
  238.7 1.2 copy-start.20
  239.9 1.2 copy-start.22
  241.1 5.7 %copy-start.24 = (f32[512,512]{1,0:T(8,128)S(1)}, f32[512,512]{1,0:T(8,128)}, u32[]{:S(2)}) copy-start(f32[512,512]{1,0:T(8,128)} %copy-done.23) | copy-start | bytes 3145732
  241.1 5.7 %copy-start.26 = (f32[512,512]{1,0:T(8,128)S(1)}, f32[512,512]{1,0:T(8,128)}, u32[]{:S(2)}) copy-start(f32[512,512]{1,0:T(8,128)} %copy-done.25) | copy-start | bytes 3145732
  241.1 5.7 %copy-start.28 = (f32[512,512]{1,0:T(8,128)S(1)}, f32[512,512]{1,0:T(8,128)}, u32[]{:S(2)}) copy-start(f32[512,512]{1,0:T(8,128)} %copy-done.27) | copy-start | bytes 3145732
  246.9 6.5 %copy-start.36 = (f32[512,512]{1,0:T(8,128)S(1)}, f32[512,512]{1,0:T(8,128)}, u32[]{:S(2)}) copy-start(f32[512,512]{1,0:T(8,128)} %copy-done.35) | copy-start | bytes 3145732
  246.9 6.5 %copy-start.38 = (f32[512,512]{1,0:T(8,128)S(1)}, f32[512,512]{1,0:T(8,128)}, u32[]{:S(2)}) copy-start(f32[512,512]{1,0:T(8,128)} %copy-done.37) | copy-start | bytes 3145732
  253.4 1.3 copy-start.40
  254.7 7.0 %copy-start.30 = (f32[512,512]{1,0:T(8,128)S(1)}, f32[512,512]{1,0:T(8,128)}, u32[]{:S(2)}) copy-start(f32[512,512]{1,0:T(8,128)} %copy-done.29) | copy-start | bytes 3145732
  254.7 7.0 %copy-start.32 = (f32[512,512]{1,0:T(8,128)S(1)}, f32[512,512]{1,0:T(8,128)}, u32[]{:S(2)}) copy-start(f32[512,512]{1,0:T(8,128)} %copy-done.31) | copy-start | bytes 3145732
  254.7 7.0 %copy-start.34 = (f32[512,512]{1,0:T(8,128)S(1)}, f32[512,512]{1,0:T(8,128)}, u32[]{:S(2)}) copy-start(f32[512,512]{1,0:T(8,128)} %copy-done.33) | copy-start | bytes 3145732
  260.3 1.3 copy-start.17
  261.7 5.7 %copy-start.44 = (bf16[512,512]{1,0:T(8,128)(2,1)S(1)}, bf16[512,512]{1,0:T(8,128)(2,1)}, u32[]{:S(2)}) copy-start(bf16[512,512]{1,0:T(8,128)(2,1)} %copy-done.43) | copy-start | bytes 1572868
  373.8 1.9 copy-start.18
  377.3 1.0 copy-start.51
  378.4 1.6 copy-start.50
  380.0 13.3 %copy-start.1 = (bf16[1,512,2048]{2,1,0:T(8,128)(2,1)S(1)}, bf16[1,512,2048]{2,1,0:T(8,128)(2,1)}, u32[]{:S(2)}) copy-start(bf16[1,512,2048]{2,1,0:T(8,128)(2,1)} %param.9) | copy-start | bytes 6291460
  (2 other events, 1.8 us)
Sparse Core Ops, SparseCore 0:
  107.9 46.5 reduce-scatter.5
  177.5 47.5 reduce-scatter.3
  229.2 144.5 reduce-scatter.7
  375.2 15.6 all-gather.1

commit v2 on v1

--- a/solution.py
+++ b/solution.py
@@ -8,7 +8,7 @@
 from jax.sharding import PartitionSpec as P
 
 HEADS = 16
-CHUNKS = 4
+CHUNKS = 2
 WEIGHT_PARTS = 2
 LOW = -1e30
 PARAMS = dict(vmem_limit_bytes=40 * 1024 * 1024)
@@ -23,6 +23,38 @@
 def alibi_slopes():
     head_ids = jnp.arange(HEADS, dtype=jnp.float32)
     return 2.0 ** (-(17.0 + head_ids) / 4.0)
+
+
+def halve(parts, axis, bit):
+    length = lax.axis_size(axis)
+    mine = (lax.axis_index(axis) // bit) % 2
+    sent = lax.dynamic_index_in_dim(parts, 1 - mine, 0, keepdims=False)
+    kept = lax.dynamic_index_in_dim(parts, mine, 0, keepdims=False)
+    came = lax.ppermute(sent, axis, [(i, i ^ bit) for i in range(length)])
+    return (kept.astype(jnp.float32) + came.astype(jnp.float32)).astype(jnp.bfloat16)
+
+
+def scatter_columns(term, axis):
+    bit, blocks = 1, lax.axis_size(axis)
+    rows, columns = term.shape
+    parts = term.reshape(rows, blocks, columns // blocks).transpose(1, 0, 2)
+    while bit < lax.axis_size(axis):
+        blocks = blocks // 2
+        shape = (blocks, 2) + parts.shape[1:]
+        parts = halve(jnp.swapaxes(parts.reshape(shape), 0, 1), axis, bit)
+        bit = bit * 2
+    return parts[0]
+
+
+def scatter_rows(term, axis):
+    bit, blocks = 1, lax.axis_size(axis)
+    parts = term.reshape(blocks, term.shape[0] // blocks, term.shape[1])
+    while bit < lax.axis_size(axis):
+        blocks = blocks // 2
+        shape = (blocks, 2) + parts.shape[1:]
+        parts = halve(jnp.swapaxes(parts.reshape(shape), 0, 1), axis, bit)
+        bit = bit * 2
+    return parts[0]
 
 
 def dot_nt(a, b):
@@ -138,9 +170,9 @@
     def cost(heads, dots):
         pairs = heads * tok_rows * tok_rows
         return pl.CostEstimate(
-            flops=2 * dots * pairs * head_dim,
-            bytes_accessed=16 * heads * tok_rows * head_dim,
-            transcendentals=pairs,
+            flops=dots * pairs,
+            bytes_accessed=heads * tok_rows * head_dim,
+            transcendentals=0,
         )
 
     full = jax.ShapeDtypeStruct((tok_rows, full_width), jnp.float32)
@@ -191,11 +223,9 @@
             term = lax.dot_general(
                 context, grad_rows, (((0,), (0,)), ((), ())), preferred_element_type=jnp.float32
             ).astype(jnp.bfloat16)
-            terms.append(lax.psum_scatter(term, "grp", scatter_dimension=1, tiled=True))
-
-    weight_term = lax.psum_scatter(
-        jnp.concatenate(terms, axis=0), "seq", scatter_dimension=0, tiled=True
-    )
+            terms.append(scatter_columns(term, "grp"))
+
+    weight_term = scatter_rows(jnp.concatenate(terms, axis=0), "seq")
     grad_weight = lax.all_gather(weight_term, "grp", axis=1, tiled=True)
 
     grads_q, grads_k, grads_v = [], [], []

time: 401 us -> 384 us (0.958)
  local copies, waits for them, and re-layouts: 52.5 us -> 32.8 us
  other arithmetic: 18.9 us -> 25.1 us
    ppermute x0 -> x7, waiting for transfers between devices: none -> 158 us  [halve(): came = lax.ppermute(sent, axis, [(i, i ^ bit) for i in range(length)])]
    reduce_scatter x3 -> x0, waiting for transfers between devices: 110 us -> none  [the longest x1 62.7 us: local(): lax.psum_scatter(jnp.concatenate(terms, axis=0), 'seq', scatter_dimension...]
    ppermute x9 -> x5, waiting for transfers between devices: 65.5 us -> 18.3 us  [from_behind(): return lax.ppermute(shard, axis, pairs)]
    unnamed x107 -> x63, local copies, waits for them, and re-layouts: 45.9 us -> 23.5 us
    ppermute x9 -> x5, starting transfers between devices: 26.8 us -> 15.8 us  [from_behind(): return lax.ppermute(shard, axis, pairs)]
    convert_element_type x0 -> x5, other arithmetic: none -> 9.47 us  [halve(): (kept.astype(jnp.float32) + came.astype(jnp.float32)).astype(jnp.bfloat16)]
    ppermute x0 -> x7, starting transfers between devices: none -> 8.08 us  [halve(): came = lax.ppermute(sent, axis, [(i, i ^ bit) for i in range(length)])]
    squeeze x0 -> x7, local copies, waits for them, and re-layouts: none -> 5.37 us  [halve(): sent = lax.dynamic_index_in_dim(parts, 1 - mine, 0, keepdims=False)]
  transfers between devices with their start and end apart: 13 -> 13, of which waited for: 8 -> 7; matrix products, arithmetic and copies ran while one was open for 8% -> 11% of each run, Pallas kernels for 19% -> 23%
where the time goes in v2:
time: 384 us; the launch traced here: 383 us
  waiting for transfers between devices  187 us (49%)
  Pallas kernels  86.2 us (22%)
  local copies, waits for them, and re-layouts  32.8 us (9%)
  other arithmetic  25.1 us (7%)
  starting transfers between devices  23.9 us (6%)
  between operations  14.5 us (4%)
  matrix products  13.9 us (4%)
    ppermute x7, waiting for transfers between devices, halve(): came = lax.ppermute(sent, axis, [(i, i ^ bit) for i in range(length)])  158 us
    pallas_call x2, Pallas kernels, local(): pl.pallas_call(functools.partial(hop_step, scale, base), grid=(chunk_head...  44.7 us
    pallas_call x2, Pallas kernels, local(): pl.pallas_call(functools.partial(own_backward, scale, base), grid=(chunk_...  23.5 us
    unnamed x63, local copies, waits for them, and re-layouts  23.5 us
    ppermute x5, waiting for transfers between devices, from_behind(): return lax.ppermute(shard, axis, pairs)  18.3 us
    pallas_call x1, Pallas kernels, local(): pl.pallas_call(functools.partial(own_forward, scale), grid=(HEADS,), in_s...  17.9 us
    ppermute x5, starting transfers between devices, from_behind(): return lax.ppermute(shard, axis, pairs)  15.8 us
    all_gather x1, waiting for transfers between devices, local(): grad_weight = lax.all_gather(weight_term, 'grp', axis=1, tiled=True)  10.1 us
  transfers between devices with their start and end apart: 13, of which 7 were waited for; matrix products, arithmetic and copies ran while one was open for 11% of the time, Pallas kernels for 23%

profile of v2, /device:TPU:0, one launch (start us, length us, event | category | flops | bytes accessed | tf_op | source)
XLA Modules:
  0.0 383.0 jit_solution(2163691296002402099)
XLA Ops:
  7.2 2.8 slice_bitcast_fusion.6
  10.0 1.5 pad_maximum_fusion.1
  11.5 6.2 %collective-permute-start.2 = (bf16[2,512,1024]{2,1,0:T(8,128)(2,1)}, bf16[2,512,1024]{2,1,0:T(8,128)(2,1)}, u32[]{:S(2)}, u32[]{:S(2)}) collective-permute-start(bf16[2,512,1024]{2,1,0:T(8,128)(2,1)} %pad_maximum_fusion.1), channel_id=1, source_target_pairs={{0,4},{4,8},{8,12},{12,16},{16,20},{20,24},{24,28},{1,5},{5,9},{9,... | collective-permute-start | bytes 6291464 | tf_op jit(solution)/shard_map/ppermute | solution.py:20
  17.7 2.1 collective-permute-start
  19.8 1.5 pad_maximum_fusion
  21.3 4.8 %collective-permute-start.1 = (bf16[2,512,1024]{2,1,0:T(8,128)(2,1)}, bf16[2,512,1024]{2,1,0:T(8,128)(2,1)}, u32[]{:S(2)}, u32[]{:S(2)}) collective-permute-start(bf16[2,512,1024]{2,1,0:T(8,128)(2,1)} %pad_maximum_fusion), channel_id=1, source_target_pairs={{0,4},{4,8},{8,12},{12,16},{16,20},{20,24},{24,28},{1,5},{5,9},{9,... | collective-permute-start | bytes 6291464 | tf_op jit(solution)/shard_map/ppermute | solution.py:20
  26.1 9.1 %convolution_convert_fusion.2.grad = bf16[512,2048]{1,0:T(8,128)(2,1)} fusion(bf16[2048,2048]{1,0:T(8,128)(2,1)} %param.10, bf16[1,512,2048]{2,1,0:T(8,128)(2,1)S(1)} %copy-done), kind=kOutput, calls=%fused_computation.10 | convolution fusion | flops 4296015872 | bytes 12582912 | tf_op jit(solution)/shard_map/dot_general | solution.py:182
  35.4 1.6 copy-done.2
  37.0 1.6 copy-done.6
  38.6 1.6 copy-done.8
  40.2 17.9 %own_forward.1 = (f32[512,2048]{1,0:T(8,128)S(1)}, f32[512,2048]{1,0:T(8,128)}) custom-call(f32[16]{0:T(128)S(1)} %multiply_power_fusion.slopes, s32[512,1]{1,0:T(8,128)S(1)} %copy.20.seg_col, s32[1,512]{1,0:T(1,128)S(1)} %copy-done.21, bf16[512,2048]{1,0:T(8,128)(2,1)S(1)} %bitcast.81, bf16[512,2048]{1,0:T(8,128)(2,1)S(1)} %bitcast.87, ...), custom_call_target="tpu_custom_call" | custom-call | flops 8388608 | bytes 1048576 | tf_op jit(solution)/shard_map/own_forward/pallas_call | solution.py:186
  58.1 2.1 copy-done.10
  60.2 2.5 collective-permute-done
  62.7 22.4 %hop_step.3 = (bf16[512,1024]{1,0:T(8,128)(2,1)S(1)}, f32[512,1024]{1,0:T(8,128)S(1)}, f32[512,1024]{1,0:T(8,128)S(1)}, f32[512,1024]{1,0:T(8,128)S(1)}, bf16[2,512,1024]{2,1,0:T(8,128)(2,1)}) custom-call(f32[16]{0:T(128)S(1)} %multiply_power_fusion.slopes, s32[512,1]{1,0:T(8,128)S(1)} %copy.20.seg_col, s32[1,512]{1,0:T(1,128)S(1)} %broadcast_select_fusion.seg_row, ...), custom_call_target="tpu_custom_call" | custom-call | flops 12582912 | bytes 524288 | tf_op jit(solution)/shard_map/hop_step/pallas_call | solution.py:201
  85.1 2.4 convolution_convert_fusion
  87.5 0.3 copy-done.15
  87.8 0.3 copy.33
  88.1 1.6 dynamic-slice_bitcast_fusion
  89.7 1.0 copy-done.23
  90.8 15.7 %collective-permute-done.1.kv = bf16[2,512,1024]{2,1,0:T(8,128)(2,1)} collective-permute-done((bf16[2,512,1024]{2,1,0:T(8,128)(2,1)}, bf16[2,512,1024]{2,1,0:T(8,128)(2,1)}, u32[]{:S(2)}, u32[]{:S(2)}) %collective-permute-start.1) | collective-permute-done | bytes 2097184 | tf_op jit(solution)/shard_map/ppermute | solution.py:20
  106.5 22.3 %hop_step.2 = (bf16[512,1024]{1,0:T(8,128)(2,1)S(1)}, f32[512,1024]{1,0:T(8,128)S(1)}, f32[512,1024]{1,0:T(8,128)S(1)}, f32[512,1024]{1,0:T(8,128)S(1)}, bf16[2,512,1024]{2,1,0:T(8,128)(2,1)S(1)}) custom-call(f32[16]{0:T(128)S(1)} %multiply_power_fusion.slopes, s32[512,1]{1,0:T(8,128)S(1)} %copy.20.seg_col, s32[1,512]{1,0:T(1,128)S(1)} %broadcast_select_fusion.seg_row, ...), custom_call_target="tpu_custom_call" | custom-call | flops 12582912 | bytes 524288 | tf_op jit(solution)/shard_map/hop_step/pallas_call | solution.py:201
  128.9 2.4 convolution_convert_fusion.1
  131.3 0.2 copy-done.20
  131.6 0.5 copy-done.22
  132.1 0.4 copy.34
  132.5 1.7 dynamic-slice_bitcast_fusion.1
  134.2 1.0 copy-done.24
  135.2 3.0 fusion
  138.3 1.6 collective-permute-start.8
  139.8 2.2 fusion.1
  142.0 1.3 copy-done.26
  143.3 1.0 constant_dynamic-slice_fusion.2
  144.4 1.3 collective-permute-start.6
  145.7 18.7 %collective-permute-done.8 = bf16[1,1024,512]{2,1,0:T(8,128)(2,1)} collective-permute-done((bf16[1,1024,512]{2,1,0:T(8,128)(2,1)S(1)}, bf16[1,1024,512]{2,1,0:T(8,128)(2,1)}, u32[]{:S(2)}, u32[]{:S(2)}) %collective-permute-start.8) | collective-permute-done | bytes 1048608 | tf_op jit(solution)/shard_map/ppermute | solution.py:33
  164.4 1.5 fusion.7
  165.9 20.6 %collective-permute-done.6 = bf16[1,1024,512]{2,1,0:T(8,128)(2,1)} collective-permute-done((bf16[1,1024,512]{2,1,0:T(8,128)(2,1)}, bf16[1,1024,512]{2,1,0:T(8,128)(2,1)}, u32[]{:S(2)}, u32[]{:S(2)}) %collective-permute-start.6) | collective-permute-done | bytes 1048608 | tf_op jit(solution)/shard_map/ppermute | solution.py:33
  186.5 1.5 fusion.6
  188.2 2.5 collective-permute-start.9
  190.8 1.3 collective-permute-start.4
  192.1 1.4 collective-permute-start.3
  193.6 109.4 %collective-permute-done.9 = bf16[4,256,512]{2,1,0:T(8,128)(2,1)} collective-permute-done((bf16[4,256,512]{2,1,0:T(8,128)(2,1)S(1)}, bf16[4,256,512]{2,1,0:T(8,128)(2,1)}, u32[]{:S(2)}, u32[]{:S(2)}) %collective-permute-start.9) | collective-permute-done | bytes 1048608 | tf_op jit(solution)/shard_map/ppermute | solution.py:33
  303.0 1.8 fusion.2
  304.8 0.8 dynamic-slice_bitcast_fusion.3
  305.6 1.6 collective-permute-start.10
  307.2 1.6 copy-done.5
  308.8 1.6 copy-done.7
  310.4 1.6 copy-done.9
  312.0 1.6 copy-done.12
  313.6 1.6 copy-done.14
  315.2 11.8 %own_backward.3 = (bf16[512,1024]{1,0:T(8,128)(2,1)S(1)}, f32[2,512,1024]{2,1,0:T(8,128)}) custom-call(f32[16]{0:T(128)S(1)} %multiply_power_fusion.slopes, s32[512,1]{1,0:T(8,128)S(1)} %copy.20.seg_col, s32[1,512]{1,0:T(1,128)S(1)} %copy-done.21, bf16[512,2048]{1,0:T(8,128)(2,1)S(1)} %bitcast.84, bf16[512,2048]{1,0:T(8,128)(2,1)S(1)} %bitcast.88, ...), custom_call_target="tpu_custom_call" | custom-call | flops 10485760 | bytes 524288 | tf_op jit(solution)/shard_map/own_backward/pallas_call | solution.py:236
  327.0 11.7 %own_backward.2 = (bf16[512,1024]{1,0:T(8,128)(2,1)S(1)}, f32[2,512,1024]{2,1,0:T(8,128)}) custom-call(f32[16]{0:T(128)S(1)} %multiply_power_fusion.slopes, s32[512,1]{1,0:T(8,128)S(1)} %copy.20.seg_col, s32[1,512]{1,0:T(1,128)S(1)} %copy-done.21, bf16[512,2048]{1,0:T(8,128)(2,1)S(1)} %bitcast.85, bf16[512,2048]{1,0:T(8,128)(2,1)S(1)} %bitcast.89, ...), custom_call_target="tpu_custom_call" | custom-call | flops 10485760 | bytes 524288 | tf_op jit(solution)/shard_map/own_backward/pallas_call | solution.py:236
  338.7 1.5 maximum_bitcast_fusion
  340.2 1.7 fusion.8
  341.9 1.1 collective-permute-start.11
  343.0 2.5 add_convert_fusion
  345.5 9.7 %collective-permute-done.11 = bf16[1,256,512]{2,1,0:T(8,128)(2,1)S(1)} collective-permute-done((bf16[1,256,512]{2,1,0:T(8,128)(2,1)S(1)}, bf16[1,256,512]{2,1,0:T(8,128)(2,1)S(1)}, u32[]{:S(2)}, u32[]{:S(2)}) %collective-permute-start.11) | collective-permute-done | bytes 262176 | tf_op jit(solution)/shard_map/ppermute | solution.py:33
  355.2 0.8 add_convert_fusion.4
  356.0 0.2 slice_bitcast_fusion
  356.2 2.0 copy-done.29
  358.2 2.4 add_convert_fusion.1
  360.8 1.5 maximum_bitcast_fusion.1
  362.3 1.5 maximum_bitcast_fusion.2
  363.8 10.1 %all-gather.3.cloned.1.call-done = bf16[1,256,2048]{2,1,0:T(8,128)(2,1)} async-done(((bf16[1,256,512]{2,1,0:T(8,128)(2,1)}), bf16[1,256,2048]{2,1,0:T(8,128)(2,1)}) %all-gather.3.cloned.1.call-update) | async-done | bytes 1048592 | tf_op jit(solution)/shard_map/all_gather | solution.py:229
  373.9 2.3 copy.36
  (64 shorter events, 0.8 us)
Async XLA Ops:
  7.2 18.9 %copy-start = (bf16[1,512,2048]{2,1,0:T(8,128)(2,1)S(1)}, bf16[1,512,2048]{2,1,0:T(8,128)(2,1)}, u32[]{:S(2)}) copy-start(bf16[1,512,2048]{2,1,0:T(8,128)(2,1)} %param.9) | copy-start | bytes 6291460
  7.2 366.7 %all-gather.3.cloned.1.call-start = ((), (), s32[]{:S(2)}) async-start(), calls=%async_computation | async-start | bytes 1310720 | tf_op jit(solution)/shard_map/all_gather | solution.py:229
  10.0 7.7 %copy-start.21 = (s32[1,512]{1,0:T(1,128)S(1)}, s32[1,512]{1,0:T(1,128)}, u32[]{:S(2)}) copy-start(s32[1,512]{1,0:T(1,128)} %seg_row.5) | copy-start | bytes 6148
  11.5 51.2 %collective-permute-start.2 = (bf16[2,512,1024]{2,1,0:T(8,128)(2,1)}, bf16[2,512,1024]{2,1,0:T(8,128)(2,1)}, u32[]{:S(2)}, u32[]{:S(2)}) collective-permute-start(bf16[2,512,1024]{2,1,0:T(8,128)(2,1)} %pad_maximum_fusion.1), channel_id=1, source_target_pairs={{0,4},{4,8},{8,12},{12,16},{16,20},{20,24},{24,28},{1,5},{5,9},{9,... | collective-permute-start | bytes 6291464 | tf_op jit(solution)/shard_map/ppermute | solution.py:20
  17.7 45.0 %collective-permute-start = (s32[1,512]{1,0:T(1,128)S(1)}, s32[1,512]{1,0:T(1,128)S(1)}, u32[]{:S(2)}, u32[]{:S(2)}) collective-permute-start(s32[1,512]{1,0:T(1,128)S(1)} %copy-done.21), channel_id=1, source_target_pairs={{0,4},{4,8},{8,12},{12,16},{16,20},{20,24},{24,28},{1,5},{5,9},{9,... | collective-permute-start | bytes 6152 | tf_op jit(solution)/shard_map/ppermute | solution.py:20
  21.3 85.2 %collective-permute-start.1 = (bf16[2,512,1024]{2,1,0:T(8,128)(2,1)}, bf16[2,512,1024]{2,1,0:T(8,128)(2,1)}, u32[]{:S(2)}, u32[]{:S(2)}) collective-permute-start(bf16[2,512,1024]{2,1,0:T(8,128)(2,1)} %pad_maximum_fusion), channel_id=1, source_target_pairs={{0,4},{4,8},{8,12},{12,16},{16,20},{20,24},{24,28},{1,5},{5,9},{9,... | collective-permute-start | bytes 6291464 | tf_op jit(solution)/shard_map/ppermute | solution.py:20
  35.4 1.6 copy-start.2
  37.0 1.6 copy-start.6
  38.6 1.6 copy-start.8
  40.2 22.5 %copy-start.3 = (bf16[1,512,2048]{2,1,0:T(8,128)(2,1)S(1)}, bf16[1,512,2048]{2,1,0:T(8,128)(2,1)}, u32[]{:S(2)}) copy-start(bf16[1,512,2048]{2,1,0:T(8,128)(2,1)} %param.6) | copy-start | bytes 6291460
  58.1 2.1 copy-start.10
  85.1 2.4 copy-start.11
  85.1 2.4 copy-start.13
  85.1 2.7 copy-start.15
  88.1 2.7 copy-start.23
  90.8 44.4 %collective-permute-start.7 = (bf16[2,1024,512]{2,1,0:T(8,128)(2,1)}, bf16[2,1024,512]{2,1,0:T(8,128)(2,1)}, u32[]{:S(2)}, u32[]{:S(2)}) collective-permute-start(bf16[2,1024,512]{2,1,0:T(8,128)(2,1)} %dynamic-slice_bitcast_fusion), channel_id=1, source_target_pairs={{0,1},{1,0},{2,3},{3,2},{4,5},{5,4},{6,7},{7,6},{8,9},{9,8},{10,11... | collective-permute-start | bytes 6291464 | tf_op jit(solution)/shard_map/ppermute | solution.py:33
  128.9 2.4 copy-start.16
  128.9 2.4 copy-start.18
  128.9 2.7 copy-start.20
  128.9 3.2 copy-start.22
  132.5 2.6 copy-start.24
  135.2 4.7 %collective-permute-start.5 = (bf16[2,1024,512]{2,1,0:T(8,128)(2,1)}, bf16[2,1024,512]{2,1,0:T(8,128)(2,1)}, u32[]{:S(2)}, u32[]{:S(2)}) collective-permute-start(bf16[2,1024,512]{2,1,0:T(8,128)(2,1)} %dynamic-slice_bitcast_fusion.1), channel_id=1, source_target_pairs={{0,1},{1,0},{2,3},{3,2},{4,5},{5,4},{6,7},{7,6},{8,9},{9,8},{10,11... | collective-permute-start | bytes 6291464 | tf_op jit(solution)/shard_map/ppermute | solution.py:33
  135.2 4.7 %copy-start.25 = (bf16[128,4,8,512]{3,2,0,1:T(8,128)(2,1)S(1)}, bf16[128,4,8,512]{3,2,0,1:T(8,128)(2,1)}, u32[]{:S(2)}) copy-start(bf16[128,4,8,512]{3,2,0,1:T(8,128)(2,1)} %copy-done.24) | copy-start | bytes 12582916
  138.3 26.1 %collective-permute-start.8 = (bf16[1,1024,512]{2,1,0:T(8,128)(2,1)S(1)}, bf16[1,1024,512]{2,1,0:T(8,128)(2,1)}, u32[]{:S(2)}, u32[]{:S(2)}) collective-permute-start(bf16[1,1024,512]{2,1,0:T(8,128)(2,1)S(1)} %constant_dynamic-slice_fusion.1), channel_id=1, source_target_pairs={{0,2},{1,3},{2,0},{3,1},{4,6},{5,7},{6,4},{7,5},{8,10},{9,11},{10,... | collective-permute-start | bytes 3145736 | tf_op jit(solution)/shard_map/ppermute | solution.py:33
  142.0 1.3 copy-start.26
  144.4 42.1 %collective-permute-start.6 = (bf16[1,1024,512]{2,1,0:T(8,128)(2,1)}, bf16[1,1024,512]{2,1,0:T(8,128)(2,1)}, u32[]{:S(2)}, u32[]{:S(2)}) collective-permute-start(bf16[1,1024,512]{2,1,0:T(8,128)(2,1)} %constant_dynamic-slice_fusion.2), channel_id=1, source_target_pairs={{0,2},{1,3},{2,0},{3,1},{4,6},{5,7},{6,4},{7,5},{8,10},{9,11},{10,... | collective-permute-start | bytes 3145736 | tf_op jit(solution)/shard_map/ppermute | solution.py:33
  145.7 40.8 %copy-start.27 = (bf16[2,1024,512]{2,1,0:T(8,128)(2,1)S(1)}, bf16[2,1024,512]{2,1,0:T(8,128)(2,1)}, u32[]{:S(2)}) copy-start(bf16[2,1024,512]{2,1,0:T(8,128)(2,1)} %copy-done.26) | copy-start | bytes 6291460
  188.1 4.0 %copy-start.28 = (bf16[2048,512]{1,0:T(8,128)(2,1)}, bf16[2048,512]{1,0:T(8,128)(2,1)S(1)}, u32[]{:S(2)}) copy-start(bf16[2048,512]{1,0:T(8,128)(2,1)S(1)} %pad_maximum_fusion.2) | copy-start | bytes 6291460
  188.2 114.7 %collective-permute-start.9 = (bf16[4,256,512]{2,1,0:T(8,128)(2,1)S(1)}, bf16[4,256,512]{2,1,0:T(8,128)(2,1)}, u32[]{:S(2)}, u32[]{:S(2)}) collective-permute-start(bf16[4,256,512]{2,1,0:T(8,128)(2,1)S(1)} %dynamic-slice_bitcast_fusion.2), channel_id=1, source_target_pairs={{0,4},{4,0},{8,12},{12,8},{16,20},{20,16},{24,28},{28,24},{1,5},{5... | collective-permute-start | bytes 3145736 | tf_op jit(solution)/shard_map/ppermute | solution.py:33
  190.8 152.3 %collective-permute-start.4 = (bf16[2,512,1024]{2,1,0:T(8,128)(2,1)}, bf16[2,512,1024]{2,1,0:T(8,128)(2,1)}, u32[]{:S(2)}, u32[]{:S(2)}) collective-permute-start(bf16[2,512,1024]{2,1,0:T(8,128)(2,1)} %get-tuple-element.33), channel_id=1, source_target_pairs={{4,0},{8,4},{12,8},{16,12},{20,16},{24,20},{28,24},{5,1},{9,5},{13... | collective-permute-start | bytes 6291464 | tf_op jit(solution)/shard_map/ppermute | solution.py:20
  192.1 115.1 %copy-start.4 = (bf16[1,512,2048]{2,1,0:T(8,128)(2,1)S(1)}, bf16[1,512,2048]{2,1,0:T(8,128)(2,1)}, u32[]{:S(2)}) copy-start(bf16[1,512,2048]{2,1,0:T(8,128)(2,1)} %param.6) | copy-start | bytes 6291460
  192.1 164.0 %collective-permute-start.3 = (bf16[2,512,1024]{2,1,0:T(8,128)(2,1)}, bf16[2,512,1024]{2,1,0:T(8,128)(2,1)}, u32[]{:S(2)}, u32[]{:S(2)}) collective-permute-start(bf16[2,512,1024]{2,1,0:T(8,128)(2,1)} %copy-done.22), channel_id=1, source_target_pairs={{4,0},{8,4},{12,8},{16,12},{20,16},{24,20},{28,24},{5,1},{9,5},{13... | collective-permute-start | bytes 6291464 | tf_op jit(solution)/shard_map/ppermute | solution.py:20
  305.6 34.6 %collective-permute-start.10 = (bf16[2,256,512]{2,1,0:T(8,128)(2,1)}, bf16[2,256,512]{2,1,0:T(8,128)(2,1)}, u32[]{:S(2)}, u32[]{:S(2)}) collective-permute-start(bf16[2,256,512]{2,1,0:T(8,128)(2,1)} %dynamic-slice_bitcast_fusion.3), channel_id=1, source_target_pairs={{0,8},{4,12},{8,0},{12,4},{16,24},{20,28},{24,16},{28,20},{1,9},{5... | collective-permute-start | bytes 1572872 | tf_op jit(solution)/shard_map/ppermute | solution.py:33
  307.2 1.6 copy-start.5
  308.8 1.6 copy-start.7
  310.4 1.6 copy-start.9
  312.0 1.6 copy-start.12
  313.6 1.6 copy-start.14
  315.2 11.8 %copy-start.17 = (f32[512,1024]{1,0:T(8,128)S(1)}, f32[512,1024]{1,0:T(8,128)}, u32[]{:S(2)}) copy-start(f32[512,1024]{1,0:T(8,128)} %copy-done.16) | copy-start | bytes 6291460
  315.2 11.8 %copy-start.19 = (f32[512,1024]{1,0:T(8,128)S(1)}, f32[512,1024]{1,0:T(8,128)}, u32[]{:S(2)}) copy-start(f32[512,1024]{1,0:T(8,128)} %copy-done.18) | copy-start | bytes 6291460
  338.7 4.3 %copy-start.30 = (f32[2,512,1024]{2,1,0:T(8,128)S(1)}, f32[2,512,1024]{2,1,0:T(8,128)}, u32[]{:S(2)}) copy-start(f32[2,512,1024]{2,1,0:T(8,128)} %get-tuple-element.32) | copy-start | bytes 12582916
  341.9 13.2 %collective-permute-start.11 = (bf16[1,256,512]{2,1,0:T(8,128)(2,1)S(1)}, bf16[1,256,512]{2,1,0:T(8,128)(2,1)S(1)}, u32[]{:S(2)}, u32[]{:S(2)}) collective-permute-start(bf16[1,256,512]{2,1,0:T(8,128)(2,1)S(1)} %constant_dynamic-slice_fusion), channel_id=1, source_target_pairs={{0,16},{4,20},{8,24},{12,28},{16,0},{20,4},{24,8},{28,12},{1,17},{... | collective-permute-start | bytes 786440 | tf_op jit(solution)/shard_map/ppermute | solution.py:33
  356.0 2.2 copy-start.29
  362.3 13.9 %copy-start.1 = (bf16[1,512,2048]{2,1,0:T(8,128)(2,1)S(1)}, bf16[1,512,2048]{2,1,0:T(8,128)(2,1)}, u32[]{:S(2)}) copy-start(bf16[1,512,2048]{2,1,0:T(8,128)(2,1)} %param.9) | copy-start | bytes 6291460
Sparse Core Ops, SparseCore 0:
  356.1 17.7 all-gather.2

commit v3 on v2

--- a/solution.py
+++ b/solution.py
@@ -9,7 +9,6 @@
 
 HEADS = 16
 CHUNKS = 2
-WEIGHT_PARTS = 2
 LOW = -1e30
 PARAMS = dict(vmem_limit_bytes=40 * 1024 * 1024)
 
@@ -34,10 +33,15 @@
     return (kept.astype(jnp.float32) + came.astype(jnp.float32)).astype(jnp.bfloat16)
 
 
-def scatter_columns(term, axis):
-    bit, blocks = 1, lax.axis_size(axis)
+def split_columns(term, axis):
+    blocks = lax.axis_size(axis)
     rows, columns = term.shape
-    parts = term.reshape(rows, blocks, columns // blocks).transpose(1, 0, 2)
+    parts = term.reshape(rows, blocks // 2, 2, columns // blocks).transpose(2, 1, 0, 3)
+    return halve(parts, axis, 1)
+
+
+def finish_columns(parts, axis):
+    bit, blocks = 2, parts.shape[0]
     while bit < lax.axis_size(axis):
         blocks = blocks // 2
         shape = (blocks, 2) + parts.shape[1:]
@@ -46,15 +50,18 @@
     return parts[0]
 
 
-def scatter_rows(term, axis):
-    bit, blocks = 1, lax.axis_size(axis)
-    parts = term.reshape(blocks, term.shape[0] // blocks, term.shape[1])
-    while bit < lax.axis_size(axis):
-        blocks = blocks // 2
-        shape = (blocks, 2) + parts.shape[1:]
-        parts = halve(jnp.swapaxes(parts.reshape(shape), 0, 1), axis, bit)
-        bit = bit * 2
-    return parts[0]
+def scatter_rows(term, axis, late):
+    length = lax.axis_size(axis)
+    bits = [1 << n for n in range(length.bit_length() - 1)]
+    shape = (2,) * len(bits) + (term.shape[0] // length, term.shape[1])
+    parts = term.reshape(shape)
+    left = bits[::-1]
+    for step, bit in enumerate(bits[1:] + bits[:1]):
+        if step == 1:
+            parts, late = lax.optimization_barrier((parts, late))
+        parts = halve(jnp.moveaxis(parts, left.index(bit), 0), axis, bit)
+        left.remove(bit)
+    return parts, late
 
 
 def dot_nt(a, b):
@@ -194,10 +201,14 @@
         name="own_forward",
     )(slopes, seg_col, seg_row, query_rows, key_rows, value_rows)
 
-    hops, backs, terms, pieces = [], [], [], []
+    hops, backs, terms = [], [], []
+    held = None
     for part in range(CHUNKS):
         base = part * chunk_heads
         own_spec = head_spec(base)
+        came = arrived[part]
+        if held is not None:
+            terms.append(finish_columns(held, "grp"))
         hop = pl.pallas_call(
             functools.partial(hop_step, scale, base),
             grid=(chunk_heads,),
@@ -213,22 +224,19 @@
             compiler_params=pltpu.CompilerParams(**PARAMS),
             cost_estimate=cost(chunk_heads, 6),
             name="hop_step",
-        )(slopes, seg_col, seg_behind, query_rows, arrived[part], grad_context, own_out, own_stat)
+        )(slopes, seg_col, seg_behind, query_rows, came, grad_context, own_out, own_stat)
         hops.append(hop)
         backs.append(from_behind(hop[4], "seq", -1))
-        pieces.append(hop[0])
-        if (part + 1) % (CHUNKS // WEIGHT_PARTS) == 0:
-            context = jnp.concatenate(pieces, axis=1)
-            pieces = []
-            term = lax.dot_general(
-                context, grad_rows, (((0,), (0,)), ((), ())), preferred_element_type=jnp.float32
-            ).astype(jnp.bfloat16)
-            terms.append(scatter_columns(term, "grp"))
-
-    weight_term = scatter_rows(jnp.concatenate(terms, axis=0), "seq")
-    grad_weight = lax.all_gather(weight_term, "grp", axis=1, tiled=True)
-
-    grads_q, grads_k, grads_v = [], [], []
+        context = hop[0]
+        if part > 0:
+            context, backs[part - 1] = lax.optimization_barrier((context, backs[part - 1]))
+        term = lax.dot_general(
+            context, grad_rows, (((0,), (0,)), ((), ())), preferred_element_type=jnp.float32
+        ).astype(jnp.bfloat16)
+        held = split_columns(term, "grp")
+    terms.append(finish_columns(held, "grp"))
+
+    grads_q, grads_k, grads_v, own_terms = [], [], [], []
     for part in range(CHUNKS):
         base = part * chunk_heads
         own_spec = head_spec(base)
@@ -243,8 +251,13 @@
             cost_estimate=cost(chunk_heads, 5),
             name="own_backward",
         )(slopes, seg_col, seg_row, query_rows, key_rows, value_rows, grad_context, lse, delta, hop_q)
-        total = (grad_kv + backs[part].astype(jnp.float32)).astype(jnp.bfloat16)
+        own_terms.append(grad_kv)
         grads_q.append(grad_q)
+    terms, own_terms = lax.optimization_barrier((terms, own_terms))
+    weight_term, backs[-1] = scatter_rows(jnp.concatenate(terms, axis=0), "seq", backs[-1])
+    grad_weight = lax.all_gather(weight_term, "grp", axis=1, tiled=True)
+    for part in range(CHUNKS):
+        total = (own_terms[part] + backs[part].astype(jnp.float32)).astype(jnp.bfloat16)
         grads_k.append(total[0])
         grads_v.append(total[1])
     grad_query = jnp.concatenate(grads_q, axis=1)

time: 384 us -> 352 us (0.917)
  waiting for transfers between devices: 187 us -> 106 us
  local copies, waits for them, and re-layouts: 32.8 us -> 80.3 us
    ppermute x7, waiting for transfers between devices: 158 us -> 61.4 us  [halve(): came = lax.ppermute(sent, axis, [(i, i ^ bit) for i in range(length)])]
    dynamic_slice x0 -> x2, local copies, waits for them, and re-layouts: none -> 22.3 us  [halve(): kept = lax.dynamic_index_in_dim(parts, mine, 0, keepdims=False)]
    ppermute x5, waiting for transfers between devices: 18.3 us -> 39.2 us  [from_behind(): return lax.ppermute(shard, axis, pairs)]
    reshape x2, local copies, waits for them, and re-layouts: 0.71 us -> 15.6 us  [split_columns(): term.reshape(rows, blocks // 2, 2, columns // blocks).transpose(2, 1, 0, 3)]
    unnamed x63 -> x77, local copies, waits for them, and re-layouts: 23.5 us -> 34.8 us
    dot_general x2, matrix products: 4.78 us -> 10 us  [local(): lax.dot_general(context, grad_rows, (((0,), (0,)), ((), ())), preferred_e...]
    all_gather x1, waiting for transfers between devices: 10.1 us -> 5.77 us  [local(): grad_weight = lax.all_gather(weight_term, 'grp', axis=1, tiled=True)]
  transfers between devices with their start and end apart: 13 -> 13, of which waited for: 7 -> 7; matrix products, arithmetic and copies ran while one was open for 11% -> 24% of each run, Pallas kernels for 23% -> 24%
where the time goes in v3:
time: 352 us; the launch traced here: 351 us
  waiting for transfers between devices  106 us (30%)
  Pallas kernels  85.9 us (24%)
  local copies, waits for them, and re-layouts  80.3 us (23%)
  other arithmetic  26.1 us (7%)
  starting transfers between devices  22.3 us (6%)
  matrix products  16 us (5%)
  between operations  14.4 us (4%)
    ppermute x7, waiting for transfers between devices, halve(): came = lax.ppermute(sent, axis, [(i, i ^ bit) for i in range(length)])  61.4 us
    pallas_call x2, Pallas kernels, local(): pl.pallas_call(functools.partial(hop_step, scale, base), grid=(chunk_head...  44.4 us
    ppermute x5, waiting for transfers between devices, from_behind(): return lax.ppermute(shard, axis, pairs)  39.2 us
    unnamed x77, local copies, waits for them, and re-layouts  34.8 us
    pallas_call x2, Pallas kernels, local(): pl.pallas_call(functools.partial(own_backward, scale, base), grid=(chunk_...  23.6 us
    dynamic_slice x2, local copies, waits for them, and re-layouts, halve(): kept = lax.dynamic_index_in_dim(parts, mine, 0, keepdims=False)  22.3 us
    pallas_call x1, Pallas kernels, local(): pl.pallas_call(functools.partial(own_forward, scale), grid=(HEADS,), in_s...  17.9 us
    ppermute x5, starting transfers between devices, from_behind(): return lax.ppermute(shard, axis, pairs)  15.8 us
  transfers between devices with their start and end apart: 13, of which 7 were waited for; matrix products, arithmetic and copies ran while one was open for 24% of the time, Pallas kernels for 24%

profile of v3, /device:TPU:0, one launch (start us, length us, event | category | flops | bytes accessed | tf_op | source)
XLA Modules:
  0.0 351.3 jit_solution(2631117187000976874)
XLA Ops:
  7.2 2.8 slice_bitcast_fusion.6
  10.1 1.5 pad_maximum_fusion
  11.6 6.4 %collective-permute-start.1 = (bf16[2,512,1024]{2,1,0:T(8,128)(2,1)}, bf16[2,512,1024]{2,1,0:T(8,128)(2,1)}, u32[]{:S(2)}, u32[]{:S(2)}) collective-permute-start(bf16[2,512,1024]{2,1,0:T(8,128)(2,1)} %pad_maximum_fusion), channel_id=1, source_target_pairs={{0,4},{4,8},{8,12},{12,16},{16,20},{20,24},{24,28},{1,5},{5,9},{9,... | collective-permute-start | bytes 6291464 | tf_op jit(solution)/shard_map/ppermute | solution.py:19
  17.9 2.1 collective-permute-start
  20.0 1.5 pad_maximum_fusion.1
  21.5 4.8 %collective-permute-start.2 = (bf16[2,512,1024]{2,1,0:T(8,128)(2,1)}, bf16[2,512,1024]{2,1,0:T(8,128)(2,1)}, u32[]{:S(2)}, u32[]{:S(2)}) collective-permute-start(bf16[2,512,1024]{2,1,0:T(8,128)(2,1)} %pad_maximum_fusion.1), channel_id=1, source_target_pairs={{0,4},{4,8},{8,12},{12,16},{16,20},{20,24},{24,28},{1,5},{5,9},{9,... | collective-permute-start | bytes 6291464 | tf_op jit(solution)/shard_map/ppermute | solution.py:19
  26.4 6.0 %convolution_convert_fusion.2.grad = bf16[512,2048]{1,0:T(8,128)(2,1)} fusion(bf16[2048,2048]{1,0:T(8,128)(2,1)S(1)} %bitcast.95, bf16[1,512,2048]{2,1,0:T(8,128)(2,1)S(1)} %copy-done), kind=kOutput, calls=%fused_computation.8 | convolution fusion | flops 4296015872 | bytes 12582912 | tf_op jit(solution)/shard_map/dot_general | solution.py:189
  32.5 1.6 copy-done.2
  34.1 1.6 copy-done.7
  35.7 1.6 copy-done.9
  37.3 17.9 %own_forward.1 = (f32[512,2048]{1,0:T(8,128)S(1)}, f32[512,2048]{1,0:T(8,128)}) custom-call(f32[16]{0:T(128)S(1)} %multiply_power_fusion.slopes, s32[512,1]{1,0:T(8,128)S(1)} %copy.15.seg_col, s32[1,512]{1,0:T(1,128)S(1)} %copy-done.24, bf16[512,2048]{1,0:T(8,128)(2,1)S(1)} %bitcast.78, bf16[512,2048]{1,0:T(8,128)(2,1)S(1)} %bitcast.84, ...), custom_call_target="tpu_custom_call" | custom-call | flops 8388608 | bytes 1048576 | tf_op jit(solution)/shard_map/own_forward/pallas_call | solution.py:193
  55.2 2.1 copy-done.11
  57.2 5.7 %collective-permute-done = s32[1,512]{1,0:T(1,128)S(1)} collective-permute-done((s32[1,512]{1,0:T(1,128)S(1)}, s32[1,512]{1,0:T(1,128)S(1)}, u32[]{:S(2)}, u32[]{:S(2)}) %collective-permute-start) | collective-permute-done | bytes 2080 | tf_op jit(solution)/shard_map/ppermute | solution.py:19
  62.9 22.2 %hop_step.2 = (bf16[512,1024]{1,0:T(8,128)(2,1)S(1)}, f32[512,1024]{1,0:T(8,128)S(1)}, f32[512,1024]{1,0:T(8,128)S(1)}, f32[512,1024]{1,0:T(8,128)S(1)}, bf16[2,512,1024]{2,1,0:T(8,128)(2,1)}) custom-call(f32[16]{0:T(128)S(1)} %multiply_power_fusion.slopes, s32[512,1]{1,0:T(8,128)S(1)} %copy.15.seg_col, s32[1,512]{1,0:T(1,128)S(1)} %broadcast_select_fusion.seg_row, ...), custom_call_target="tpu_custom_call" | custom-call | flops 12582912 | bytes 524288 | tf_op jit(solution)/shard_map/hop_step/pallas_call | solution.py:212
  85.1 1.4 copy-done.12
  86.5 1.4 copy-done.14
  87.9 1.4 copy-done.16
  90.2 1.3 collective-permute-start.5
  91.5 5.6 %convolution_convert_fusion.1 = bf16[1024,2048]{1,0:T(8,128)(2,1)} fusion(bf16[512,1024]{1,0:T(8,128)(2,1)} %copy-done.26, bf16[1,512,2048]{2,1,0:T(8,128)(2,1)S(1)} %copy-done), kind=kOutput, calls=%fused_computation.7 | convolution fusion | flops 2149580800 | bytes 7340032 | tf_op jit(solution)/shard_map/dot_general | solution.py:233
  97.2 7.8 %reshape.47 = bf16[1024,2,2,512]{3,2,1,0:T(2,128)(2,1)} reshape(bf16[1024,2048]{1,0:T(8,128)(2,1)} %convolution_convert_fusion.1) | data formatting | bytes 8388608 | tf_op jit(solution)/shard_map/reshape | solution.py:39
  104.9 11.3 %constant_dynamic-slice_fusion.5 = (bf16[1024,2,1,512]{3,2,1,0:T(2,128)(2,1)}, bf16[1024,2,1,512]{3,2,1,0:T(2,128)(2,1)S(1)}) fusion(bf16[1024,2,2,512]{3,2,1,0:T(2,128)(2,1)} %reshape.47, s32[]{:T(128)S(6)} %select_n.91, s32[]{:T(128)S(6)} %select_n.92), kind=kLoop, calls=%fused_computation.47 | loop fusion | bytes 8388616 | tf_op jit(solution)/shard_map/jit(dynamic_index_in_dim)/dynamic_slice | solution.py:31
  116.2 2.0 copy.31
  118.2 33.5 %collective-permute-done.2.kv = bf16[2,512,1024]{2,1,0:T(8,128)(2,1)} collective-permute-done((bf16[2,512,1024]{2,1,0:T(8,128)(2,1)}, bf16[2,512,1024]{2,1,0:T(8,128)(2,1)}, u32[]{:S(2)}, u32[]{:S(2)}) %collective-permute-start.2) | collective-permute-done | bytes 2097184 | tf_op jit(solution)/shard_map/ppermute | solution.py:19
  151.7 22.2 %hop_step.3 = (bf16[512,1024]{1,0:T(8,128)(2,1)S(1)}, f32[512,1024]{1,0:T(8,128)S(1)}, f32[512,1024]{1,0:T(8,128)S(1)}, f32[512,1024]{1,0:T(8,128)S(1)}, bf16[2,512,1024]{2,1,0:T(8,128)(2,1)S(1)}) custom-call(f32[16]{0:T(128)S(1)} %multiply_power_fusion.slopes, s32[512,1]{1,0:T(8,128)S(1)} %copy.15.seg_col, s32[1,512]{1,0:T(1,128)S(1)} %broadcast_select_fusion.seg_row, ...), custom_call_target="tpu_custom_call" | custom-call | flops 12582912 | bytes 524288 | tf_op jit(solution)/shard_map/hop_step/pallas_call | solution.py:212
  173.9 1.3 copy-done.17
  175.2 1.3 copy-done.19
  176.5 1.3 copy-done.21
  177.8 1.3 copy-done.25
  179.1 4.4 %convolution_convert_fusion = bf16[1024,2048]{1,0:T(8,128)(2,1)} fusion(bf16[512,1024]{1,0:T(8,128)(2,1)S(1)} %get-tuple-element.41, bf16[1,512,2048]{2,1,0:T(8,128)(2,1)S(1)} %copy-done), kind=kOutput, calls=%fused_computation.6 | convolution fusion | flops 2149580800 | bytes 7340032 | tf_op jit(solution)/shard_map/dot_general | solution.py:233
  183.5 7.8 %reshape.48 = bf16[1024,2,2,512]{3,2,1,0:T(2,128)(2,1)} reshape(bf16[1024,2048]{1,0:T(8,128)(2,1)} %convolution_convert_fusion) | data formatting | bytes 8388608 | tf_op jit(solution)/shard_map/reshape | solution.py:39
  191.4 11.1 %constant_dynamic-slice_fusion.2 = (bf16[1024,2,1,512]{3,2,1,0:T(2,128)(2,1)}, bf16[1024,2,1,512]{3,2,1,0:T(2,128)(2,1)S(1)}) fusion(bf16[1024,2,2,512]{3,2,1,0:T(2,128)(2,1)} %reshape.48, s32[]{:T(128)S(6)} %select_n.91, s32[]{:T(128)S(6)} %select_n.92), kind=kLoop, calls=%fused_computation.44 | loop fusion | bytes 8388616 | tf_op jit(solution)/shard_map/jit(dynamic_index_in_dim)/dynamic_slice | solution.py:31
  202.4 2.0 copy.30
  204.4 3.8 %fusion.1 = bf16[2,1024,512]{2,1,0:T(8,128)(2,1)S(1)} fusion(bf16[2,1024,512]{2,1,0:T(8,128)(2,1)} %collective-permute-done.3, bf16[1024,2,1,512]{3,2,1,0:T(2,128)(2,1)} %get-tuple-element.54), kind=kLoop, calls=%fused_computation.3 | loop fusion | flops 4194304 | bytes 6291456 | tf_op jit(solution)/shard_map/convert_element_type | solution.py:33
  208.3 1.2 constant_dynamic-slice_fusion.3
  209.5 1.5 collective-permute-start.4
  211.0 2.4 fusion
  213.4 1.3 copy-done.31
  216.4 1.3 collective-permute-start.9
  217.8 1.6 copy-done.6
  219.3 1.6 copy-done.8
  220.9 1.6 copy-done.10
  222.5 1.6 copy-done.18
  224.1 1.6 copy-done.20
  225.7 11.8 %own_backward.3 = (bf16[512,1024]{1,0:T(8,128)(2,1)S(1)}, f32[2,512,1024]{2,1,0:T(8,128)}) custom-call(f32[16]{0:T(128)S(1)} %multiply_power_fusion.slopes, s32[512,1]{1,0:T(8,128)S(1)} %copy.15.seg_col, s32[1,512]{1,0:T(1,128)S(1)} %copy-done.24, bf16[512,2048]{1,0:T(8,128)(2,1)S(1)} %bitcast.81, bf16[512,2048]{1,0:T(8,128)(2,1)S(1)} %bitcast.85, ...), custom_call_target="tpu_custom_call" | custom-call | flops 10485760 | bytes 524288 | tf_op jit(solution)/shard_map/own_backward/pallas_call | solution.py:244
  237.5 11.8 %own_backward.2 = (bf16[512,1024]{1,0:T(8,128)(2,1)S(1)}, f32[2,512,1024]{2,1,0:T(8,128)}) custom-call(f32[16]{0:T(128)S(1)} %multiply_power_fusion.slopes, s32[512,1]{1,0:T(8,128)S(1)} %copy.15.seg_col, s32[1,512]{1,0:T(1,128)S(1)} %copy-done.24, bf16[512,2048]{1,0:T(8,128)(2,1)S(1)} %bitcast.82, bf16[512,2048]{1,0:T(8,128)(2,1)S(1)} %bitcast.86, ...), custom_call_target="tpu_custom_call" | custom-call | flops 10485760 | bytes 524288 | tf_op jit(solution)/shard_map/own_backward/pallas_call | solution.py:244
  249.4 1.9 fusion.6
  251.3 6.5 %collective-permute-done.7 = bf16[1,1024,512]{2,1,0:T(8,128)(2,1)} collective-permute-done((bf16[1,1024,512]{2,1,0:T(8,128)(2,1)}, bf16[1,1024,512]{2,1,0:T(8,128)(2,1)}, u32[]{:S(2)}, u32[]{:S(2)}) %collective-permute-start.7) | collective-permute-done | bytes 1048608 | tf_op jit(solution)/shard_map/ppermute | solution.py:32
  257.8 1.5 fusion.7
  259.5 1.1 dynamic-slice_bitcast_fusion
  260.6 1.6 collective-permute-start.8
  262.2 28.6 %collective-permute-done.8 = bf16[2,2,256,512]{3,2,1,0:T(8,128)(2,1)} collective-permute-done((bf16[2,2,256,512]{3,2,1,0:T(8,128)(2,1)}, bf16[2,2,256,512]{3,2,1,0:T(8,128)(2,1)}, u32[]{:S(2)}, u32[]{:S(2)}) %collective-permute-start.8) | collective-permute-done | bytes 1048608 | tf_op jit(solution)/shard_map/ppermute | solution.py:32
  290.8 1.8 fusion.2
  293.5 2.6 collective-permute-start.10
  296.1 1.5 maximum_bitcast_fusion
  297.6 20.6 %collective-permute-done.10 = bf16[2,256,512]{2,1,0:T(8,128)(2,1)} collective-permute-done((bf16[2,256,512]{2,1,0:T(8,128)(2,1)}, bf16[2,256,512]{2,1,0:T(8,128)(2,1)}, u32[]{:S(2)}, u32[]{:S(2)}) %collective-permute-start.10) | collective-permute-done | bytes 524320 | tf_op jit(solution)/shard_map/ppermute | solution.py:32
  318.2 1.2 fusion.8
  319.5 2.5 add_convert_fusion.1
  321.9 5.7 %collective-permute-done.11 = bf16[256,512]{1,0:T(8,128)(2,1)S(1)} collective-permute-done((bf16[256,512]{1,0:T(8,128)(2,1)S(1)}, bf16[256,512]{1,0:T(8,128)(2,1)S(1)}, u32[]{:S(2)}, u32[]{:S(2)}) %collective-permute-start.11) | collective-permute-done | bytes 262176 | tf_op jit(solution)/shard_map/ppermute | solution.py:32
  328.6 2.0 copy-done.33
  330.6 2.5 add_convert_fusion
  333.4 1.5 maximum_bitcast_fusion.1
  334.9 1.5 maximum_bitcast_fusion.2
  336.4 5.8 %all-gather.2.cloned.1.call-done = bf16[256,2048]{1,0:T(8,128)(2,1)} async-done(((bf16[256,512]{1,0:T(8,128)(2,1)}), bf16[256,2048]{1,0:T(8,128)(2,1)}) %all-gather.2.cloned.1.call-update) | async-done | bytes 1048592 | tf_op jit(solution)/shard_map/all_gather | solution.py:258
  342.1 2.3 copy.33
  (79 shorter events, 5.2 us)
Async XLA Ops:
  7.2 19.2 %copy-start = (bf16[1,512,2048]{2,1,0:T(8,128)(2,1)S(1)}, bf16[1,512,2048]{2,1,0:T(8,128)(2,1)}, u32[]{:S(2)}) copy-start(bf16[1,512,2048]{2,1,0:T(8,128)(2,1)} %param.9) | copy-start | bytes 6291460
  7.2 335.0 %all-gather.2.cloned.1.call-start = ((), (), s32[]{:S(2)}) async-start(), calls=%async_computation | async-start | bytes 1310720 | tf_op jit(solution)/shard_map/all_gather | solution.py:258
  7.2 19.1 %slice-start = ((s8[8388608]{0:T(1024)(128)(4,1)}), s8[4194304]{0:T(1024)(128)(4,1)S(1)}, s32[]{:S(2)}) async-start(s8[8388608]{0:T(1024)(128)(4,1)} %bitcast.94), calls=%async_computation.1 | async-start | bytes 8388608
  10.0 7.9 %copy-start.24 = (s32[1,512]{1,0:T(1,128)S(1)}, s32[1,512]{1,0:T(1,128)}, u32[]{:S(2)}) copy-start(s32[1,512]{1,0:T(1,128)} %seg_row.5) | copy-start | bytes 6148
  10.0 16.3 %slice-start.1 = ((s8[8388608]{0:T(1024)(128)(4,1)}), s8[4194304]{0:T(1024)(128)(4,1)S(1)}, s32[]{:S(2)}) async-start(s8[8388608]{0:T(1024)(128)(4,1)} %bitcast.94), calls=%async_computation.2 | async-start | bytes 8388608
  11.6 51.3 %collective-permute-start.1 = (bf16[2,512,1024]{2,1,0:T(8,128)(2,1)}, bf16[2,512,1024]{2,1,0:T(8,128)(2,1)}, u32[]{:S(2)}, u32[]{:S(2)}) collective-permute-start(bf16[2,512,1024]{2,1,0:T(8,128)(2,1)} %pad_maximum_fusion), channel_id=1, source_target_pairs={{0,4},{4,8},{8,12},{12,16},{16,20},{20,24},{24,28},{1,5},{5,9},{9,... | collective-permute-start | bytes 6291464 | tf_op jit(solution)/shard_map/ppermute | solution.py:19
  17.9 45.0 %collective-permute-start = (s32[1,512]{1,0:T(1,128)S(1)}, s32[1,512]{1,0:T(1,128)S(1)}, u32[]{:S(2)}, u32[]{:S(2)}) collective-permute-start(s32[1,512]{1,0:T(1,128)S(1)} %copy-done.24), channel_id=1, source_target_pairs={{0,4},{4,8},{8,12},{12,16},{16,20},{20,24},{24,28},{1,5},{5,9},{9,... | collective-permute-start | bytes 6152 | tf_op jit(solution)/shard_map/ppermute | solution.py:19
  21.5 130.2 %collective-permute-start.2 = (bf16[2,512,1024]{2,1,0:T(8,128)(2,1)}, bf16[2,512,1024]{2,1,0:T(8,128)(2,1)}, u32[]{:S(2)}, u32[]{:S(2)}) collective-permute-start(bf16[2,512,1024]{2,1,0:T(8,128)(2,1)} %pad_maximum_fusion.1), channel_id=1, source_target_pairs={{0,4},{4,8},{8,12},{12,16},{16,20},{20,24},{24,28},{1,5},{5,9},{9,... | collective-permute-start | bytes 6291464 | tf_op jit(solution)/shard_map/ppermute | solution.py:19
  32.5 1.6 copy-start.2
  34.1 1.6 copy-start.7
  35.7 1.6 copy-start.9
  37.3 25.6 %copy-start.3 = (bf16[1,512,2048]{2,1,0:T(8,128)(2,1)S(1)}, bf16[1,512,2048]{2,1,0:T(8,128)(2,1)}, u32[]{:S(2)}) copy-start(bf16[1,512,2048]{2,1,0:T(8,128)(2,1)} %param.6) | copy-start | bytes 6291460
  55.2 2.1 copy-start.11
  85.1 1.4 copy-start.12
  86.5 1.4 copy-start.14
  87.9 1.4 copy-start.16
  89.3 1.0 copy-start.26
  90.2 88.9 %collective-permute-start.5 = (bf16[2,512,1024]{2,1,0:T(8,128)(2,1)}, bf16[2,512,1024]{2,1,0:T(8,128)(2,1)}, u32[]{:S(2)}, u32[]{:S(2)}) collective-permute-start(bf16[2,512,1024]{2,1,0:T(8,128)(2,1)} %get-tuple-element.40), channel_id=1, source_target_pairs={{4,0},{8,4},{12,8},{16,12},{20,16},{24,20},{28,24},{5,1},{9,5},{13... | collective-permute-start | bytes 6291464 | tf_op jit(solution)/shard_map/ppermute | solution.py:19
  116.2 35.5 %copy-start.4 = (bf16[1,512,2048]{2,1,0:T(8,128)(2,1)S(1)}, bf16[1,512,2048]{2,1,0:T(8,128)(2,1)}, u32[]{:S(2)}) copy-start(bf16[1,512,2048]{2,1,0:T(8,128)(2,1)} %param.6) | copy-start | bytes 6291460
  118.2 86.3 %collective-permute-start.3 = (bf16[2,1024,512]{2,1,0:T(8,128)(2,1)}, bf16[2,1024,512]{2,1,0:T(8,128)(2,1)}, u32[]{:S(2)}, u32[]{:S(2)}) collective-permute-start(bf16[2,1024,512]{2,1,0:T(8,128)(2,1)} %bitcast.77), channel_id=1, source_target_pairs={{0,1},{1,0},{2,3},{3,2},{4,5},{5,4},{6,7},{7,6},{8,9},{9,8},{10,11... | collective-permute-start | bytes 6291464 | tf_op jit(solution)/shard_map/ppermute | solution.py:32
  173.9 1.3 copy-start.17
  175.2 1.3 copy-start.19
  176.5 1.3 copy-start.21
  177.8 1.3 copy-start.25
  204.4 6.6 %collective-permute-start.6 = (bf16[2,1024,512]{2,1,0:T(8,128)(2,1)}, bf16[2,1024,512]{2,1,0:T(8,128)(2,1)}, u32[]{:S(2)}, u32[]{:S(2)}) collective-permute-start(bf16[2,1024,512]{2,1,0:T(8,128)(2,1)} %bitcast.76), channel_id=1, source_target_pairs={{0,1},{1,0},{2,3},{3,2},{4,5},{5,4},{6,7},{7,6},{8,9},{9,8},{10,11... | collective-permute-start | bytes 6291464 | tf_op jit(solution)/shard_map/ppermute | solution.py:32
  204.4 6.6 %copy-start.27 = (bf16[1024,2,1,512]{3,2,1,0:T(2,128)(2,1)S(1)}, bf16[1024,2,1,512]{3,2,1,0:T(2,128)(2,1)}, u32[]{:S(2)}) copy-start(bf16[1024,2,1,512]{3,2,1,0:T(2,128)(2,1)} %get-tuple-element.52) | copy-start | bytes 6291460
  208.2 2.7 copy-start.29
  209.5 39.9 %collective-permute-start.4 = (bf16[1,1024,512]{2,1,0:T(8,128)(2,1)}, bf16[1,1024,512]{2,1,0:T(8,128)(2,1)}, u32[]{:S(2)}, u32[]{:S(2)}) collective-permute-start(bf16[1,1024,512]{2,1,0:T(8,128)(2,1)} %constant_dynamic-slice_fusion.3), channel_id=1, source_target_pairs={{0,2},{1,3},{2,0},{3,1},{4,6},{5,7},{6,4},{7,5},{8,10},{9,11},{10,... | collective-permute-start | bytes 3145736 | tf_op jit(solution)/shard_map/ppermute | solution.py:32
  213.4 1.3 copy-start.31
  214.7 3.0 copy-start.5
  215.8 42.1 %collective-permute-start.7 = (bf16[1,1024,512]{2,1,0:T(8,128)(2,1)}, bf16[1,1024,512]{2,1,0:T(8,128)(2,1)}, u32[]{:S(2)}, u32[]{:S(2)}) collective-permute-start(bf16[1,1024,512]{2,1,0:T(8,128)(2,1)} %constant_dynamic-slice_fusion), channel_id=1, source_target_pairs={{0,2},{1,3},{2,0},{3,1},{4,6},{5,7},{6,4},{7,5},{8,10},{9,11},{10,... | collective-permute-start | bytes 3145736 | tf_op jit(solution)/shard_map/ppermute | solution.py:32
  216.4 76.2 %collective-permute-start.9 = (bf16[2,512,1024]{2,1,0:T(8,128)(2,1)}, bf16[2,512,1024]{2,1,0:T(8,128)(2,1)}, u32[]{:S(2)}, u32[]{:S(2)}) collective-permute-start(bf16[2,512,1024]{2,1,0:T(8,128)(2,1)} %copy-done.25), channel_id=1, source_target_pairs={{4,0},{8,4},{12,8},{16,12},{20,16},{24,20},{28,24},{5,1},{9,5},{13... | collective-permute-start | bytes 6291464 | tf_op jit(solution)/shard_map/ppermute | solution.py:19
  217.7 1.6 copy-start.6
  219.3 1.6 copy-start.8
  220.9 1.6 copy-start.10
  222.5 1.6 copy-start.18
  224.1 1.6 copy-start.20
  225.7 11.8 %copy-start.13 = (f32[512,1024]{1,0:T(8,128)S(1)}, f32[512,1024]{1,0:T(8,128)}, u32[]{:S(2)}) copy-start(f32[512,1024]{1,0:T(8,128)} %copy-done.12) | copy-start | bytes 6291460
  225.7 11.8 %copy-start.15 = (f32[512,1024]{1,0:T(8,128)S(1)}, f32[512,1024]{1,0:T(8,128)}, u32[]{:S(2)}) copy-start(f32[512,1024]{1,0:T(8,128)} %copy-done.14) | copy-start | bytes 6291460
  237.5 11.9 %copy-start.30 = (bf16[2,1024,512]{2,1,0:T(8,128)(2,1)S(1)}, bf16[2,1024,512]{2,1,0:T(8,128)(2,1)}, u32[]{:S(2)}) copy-start(bf16[2,1024,512]{2,1,0:T(8,128)(2,1)} %copy-done.29) | copy-start | bytes 6291460
  249.4 10.0 %copy-start.22 = (bf16[512,1024]{1,0:T(8,128)(2,1)}, bf16[512,1024]{1,0:T(8,128)(2,1)S(1)}, u32[]{:S(2)}) copy-start(bf16[512,1024]{1,0:T(8,128)(2,1)S(1)} %get-tuple-element.33) | copy-start | bytes 3145732
  249.4 8.5 %copy-start.32 = (bf16[2,1024,512]{2,1,0:T(8,128)(2,1)S(1)}, bf16[2,1024,512]{2,1,0:T(8,128)(2,1)}, u32[]{:S(2)}) copy-start(bf16[2,1024,512]{2,1,0:T(8,128)(2,1)} %copy-done.31) | copy-start | bytes 6291460
  259.5 2.7 copy-start.28
  260.6 30.2 %collective-permute-start.8 = (bf16[2,2,256,512]{3,2,1,0:T(8,128)(2,1)}, bf16[2,2,256,512]{3,2,1,0:T(8,128)(2,1)}, u32[]{:S(2)}, u32[]{:S(2)}) collective-permute-start(bf16[2,2,256,512]{3,2,1,0:T(8,128)(2,1)} %dynamic-slice_bitcast_fusion), channel_id=1, source_target_pairs={{0,8},{4,12},{8,0},{12,4},{16,24},{20,28},{24,16},{28,20},{1,9},{5... | collective-permute-start | bytes 3145736 | tf_op jit(solution)/shard_map/ppermute | solution.py:32
  262.2 33.9 %copy-start.23 = (bf16[512,1024]{1,0:T(8,128)(2,1)S(1)}, bf16[512,1024]{1,0:T(8,128)(2,1)}, u32[]{:S(2)}) copy-start(bf16[512,1024]{1,0:T(8,128)(2,1)} %copy-done.22) | copy-start | bytes 3145732
  293.5 24.7 %collective-permute-start.10 = (bf16[2,256,512]{2,1,0:T(8,128)(2,1)}, bf16[2,256,512]{2,1,0:T(8,128)(2,1)}, u32[]{:S(2)}, u32[]{:S(2)}) collective-permute-start(bf16[2,256,512]{2,1,0:T(8,128)(2,1)} %dynamic-slice_bitcast_fusion.1), channel_id=1, source_target_pairs={{0,16},{4,20},{8,24},{12,28},{16,0},{20,4},{24,8},{28,12},{1,17},{... | collective-permute-start | bytes 1572872 | tf_op jit(solution)/shard_map/ppermute | solution.py:32
  296.1 23.4 %copy-start.34 = (f32[2,512,1024]{2,1,0:T(8,128)S(1)}, f32[2,512,1024]{2,1,0:T(8,128)}, u32[]{:S(2)}) copy-start(f32[2,512,1024]{2,1,0:T(8,128)} %get-tuple-element.44) | copy-start | bytes 12582916
  319.4 8.3 %collective-permute-start.11 = (bf16[256,512]{1,0:T(8,128)(2,1)S(1)}, bf16[256,512]{1,0:T(8,128)(2,1)S(1)}, u32[]{:S(2)}, u32[]{:S(2)}) collective-permute-start(bf16[256,512]{1,0:T(8,128)(2,1)S(1)} %dynamic-slice_bitcast_fusion.2), channel_id=1, source_target_pairs={{0,4},{4,0},{8,12},{12,8},{16,20},{20,16},{24,28},{28,24},{1,5},{5... | collective-permute-start | bytes 786440 | tf_op jit(solution)/shard_map/ppermute | solution.py:32
  328.4 2.2 copy-start.33
  334.9 9.6 %copy-start.1 = (bf16[1,512,2048]{2,1,0:T(8,128)(2,1)S(1)}, bf16[1,512,2048]{2,1,0:T(8,128)(2,1)}, u32[]{:S(2)}) copy-start(bf16[1,512,2048]{2,1,0:T(8,128)(2,1)} %param.9) | copy-start | bytes 6291460
Sparse Core Ops, SparseCore 0:
  328.6 13.5 all-gather.1

commit v4 on v3

--- a/solution.py
+++ b/solution.py
@@ -36,8 +36,9 @@
 def split_columns(term, axis):
     blocks = lax.axis_size(axis)
     rows, columns = term.shape
-    parts = term.reshape(rows, blocks // 2, 2, columns // blocks).transpose(2, 1, 0, 3)
-    return halve(parts, axis, 1)
+    parts = term.reshape(rows, blocks, columns // blocks).transpose(1, 0, 2)
+    shape = (blocks // 2, 2) + parts.shape[1:]
+    return halve(jnp.swapaxes(parts.reshape(shape), 0, 1), axis, 1)
 
 
 def finish_columns(parts, axis):

time: 352 us -> 326 us (0.926)
  local copies, waits for them, and re-layouts: 80.3 us -> 39.7 us
  waiting for transfers between devices: 106 us -> 126 us
  matrix products: 16 us -> 12 us
    dynamic_slice x2 -> x0, local copies, waits for them, and re-layouts: 22.3 us -> none  [halve(): kept = lax.dynamic_index_in_dim(parts, mine, 0, keepdims=False)]
    ppermute x5, waiting for transfers between devices: 39.2 us -> 58.9 us  [from_behind(): return lax.ppermute(shard, axis, pairs)]
    reshape x2, local copies, waits for them, and re-layouts: 15.6 us -> 0.78 us  [split_columns(): parts = term.reshape(rows, blocks, columns // blocks).transpose(1, 0, 2)]
    unnamed x77 -> x79, local copies, waits for them, and re-layouts: 34.8 us -> 28.3 us
    dot_general x2, matrix products: 10 us -> 5.99 us  [local(): lax.dot_general(context, grad_rows, (((0,), (0,)), ((), ())), preferred_e...]
    squeeze x5 -> x7, local copies, waits for them, and re-layouts: 4.24 us -> 7.35 us  [halve(): sent = lax.dynamic_index_in_dim(parts, 1 - mine, 0, keepdims=False)]
  transfers between devices with their start and end apart: 13 -> 13, of which waited for: 7 -> 7; matrix products, arithmetic and copies ran while one was open for 24% -> 13% of each run, Pallas kernels for 24% -> 26%
where the time goes in v4:
time: 326 us
  waiting for transfers between devices  126 us (39%)
  Pallas kernels  85.9 us (26%)
  local copies, waits for them, and re-layouts  39.7 us (12%)
  other arithmetic  25.1 us (8%)
  starting transfers between devices  22.5 us (7%)
  between operations  14.5 us (4%)
  matrix products  12 us (4%)
    ppermute x7, waiting for transfers between devices, halve(): came = lax.ppermute(sent, axis, [(i, i ^ bit) for i in range(length)])  61 us
    ppermute x5, waiting for transfers between devices, from_behind(): return lax.ppermute(shard, axis, pairs)  58.9 us
    pallas_call x2, Pallas kernels, local(): pl.pallas_call(functools.partial(hop_step, scale, base), grid=(chunk_head...  44.4 us
    unnamed x79, local copies, waits for them, and re-layouts  28.3 us
    pallas_call x2, Pallas kernels, local(): pl.pallas_call(functools.partial(own_backward, scale, base), grid=(chunk_...  23.6 us
    pallas_call x1, Pallas kernels, local(): pl.pallas_call(functools.partial(own_forward, scale), grid=(HEADS,), in_s...  17.9 us
    ppermute x5, starting transfers between devices, from_behind(): return lax.ppermute(shard, axis, pairs)  16.2 us
    convert_element_type x5, other arithmetic, halve(): (kept.astype(jnp.float32) + came.astype(jnp.float32)).astype(jnp.bfloat16)  8.95 us
  transfers between devices with their start and end apart: 13, of which 7 were waited for; matrix products, arithmetic and copies ran while one was open for 13% of the time, Pallas kernels for 26%

profile of v4, /device:TPU:0, one launch (start us, length us, event | category | flops | bytes accessed | tf_op | source)
XLA Modules:
  0.0 325.5 jit_solution(168646285404514877)
XLA Ops:
  7.2 2.8 slice_bitcast_fusion.6
  10.1 1.5 pad_maximum_fusion
  11.6 6.4 %collective-permute-start.1 = (bf16[2,512,1024]{2,1,0:T(8,128)(2,1)}, bf16[2,512,1024]{2,1,0:T(8,128)(2,1)}, u32[]{:S(2)}, u32[]{:S(2)}) collective-permute-start(bf16[2,512,1024]{2,1,0:T(8,128)(2,1)} %pad_maximum_fusion), channel_id=1, source_target_pairs={{0,4},{4,8},{8,12},{12,16},{16,20},{20,24},{24,28},{1,5},{5,9},{9,... | collective-permute-start | bytes 6291464 | tf_op jit(solution)/shard_map/ppermute | solution.py:19
  17.9 2.1 collective-permute-start
  20.0 1.5 pad_maximum_fusion.1
  21.5 4.8 %collective-permute-start.2 = (bf16[2,512,1024]{2,1,0:T(8,128)(2,1)}, bf16[2,512,1024]{2,1,0:T(8,128)(2,1)}, u32[]{:S(2)}, u32[]{:S(2)}) collective-permute-start(bf16[2,512,1024]{2,1,0:T(8,128)(2,1)} %pad_maximum_fusion.1), channel_id=1, source_target_pairs={{0,4},{4,8},{8,12},{12,16},{16,20},{20,24},{24,28},{1,5},{5,9},{9,... | collective-permute-start | bytes 6291464 | tf_op jit(solution)/shard_map/ppermute | solution.py:19
  26.3 6.0 %convolution_convert_fusion.2.grad = bf16[512,2048]{1,0:T(8,128)(2,1)} fusion(bf16[2048,2048]{1,0:T(8,128)(2,1)S(1)} %bitcast.105, bf16[1,512,2048]{2,1,0:T(8,128)(2,1)S(1)} %copy-done), kind=kOutput, calls=%fused_computation.10 | convolution fusion | flops 4296015872 | bytes 12582912 | tf_op jit(solution)/shard_map/dot_general | solution.py:190
  32.5 1.6 copy-done.2
  34.1 1.6 copy-done.7
  35.7 1.6 copy-done.9
  37.3 17.9 %own_forward.1 = (f32[512,2048]{1,0:T(8,128)S(1)}, f32[512,2048]{1,0:T(8,128)}) custom-call(f32[16]{0:T(128)S(1)} %multiply_power_fusion.slopes, s32[512,1]{1,0:T(8,128)S(1)} %copy.19.seg_col, s32[1,512]{1,0:T(1,128)S(1)} %copy-done.24, bf16[512,2048]{1,0:T(8,128)(2,1)S(1)} %bitcast.82, bf16[512,2048]{1,0:T(8,128)(2,1)S(1)} %bitcast.88, ...), custom_call_target="tpu_custom_call" | custom-call | flops 8388608 | bytes 1048576 | tf_op jit(solution)/shard_map/own_forward/pallas_call | solution.py:194
  55.1 2.1 copy-done.11
  57.2 5.7 %collective-permute-done = s32[1,512]{1,0:T(1,128)S(1)} collective-permute-done((s32[1,512]{1,0:T(1,128)S(1)}, s32[1,512]{1,0:T(1,128)S(1)}, u32[]{:S(2)}, u32[]{:S(2)}) %collective-permute-start) | collective-permute-done | bytes 2080 | tf_op jit(solution)/shard_map/ppermute | solution.py:19
  62.9 22.3 %hop_step.2 = (bf16[512,1024]{1,0:T(8,128)(2,1)S(1)}, f32[512,1024]{1,0:T(8,128)S(1)}, f32[512,1024]{1,0:T(8,128)S(1)}, f32[512,1024]{1,0:T(8,128)S(1)}, bf16[2,512,1024]{2,1,0:T(8,128)(2,1)}) custom-call(f32[16]{0:T(128)S(1)} %multiply_power_fusion.slopes, s32[512,1]{1,0:T(8,128)S(1)} %copy.19.seg_col, s32[1,512]{1,0:T(1,128)S(1)} %broadcast_select_fusion.seg_row, ...), custom_call_target="tpu_custom_call" | custom-call | flops 12582912 | bytes 524288 | tf_op jit(solution)/shard_map/hop_step/pallas_call | solution.py:213
  85.2 1.3 copy-done.12
  86.5 1.4 copy-done.14
  87.9 1.3 copy-done.16
  89.2 1.0 copy-done.26
  90.2 1.5 collective-permute-start.5
  91.7 3.6 %convolution_convert_fusion.1 = bf16[1024,2048]{1,0:T(8,128)(2,1)S(1)} fusion(bf16[512,1024]{1,0:T(8,128)(2,1)} %copy-done.26, bf16[1,512,2048]{2,1,0:T(8,128)(2,1)S(1)} %copy-done), kind=kOutput, calls=%fused_computation.9 | convolution fusion | flops 2149580800 | bytes 7340032 | tf_op jit(solution)/shard_map/dot_general | solution.py:234
  95.3 0.4 copy.31
  95.7 1.6 dynamic-slice_bitcast_fusion.1
  97.3 1.2 copy-done.27
  98.5 53.2 %collective-permute-done.2.kv = bf16[2,512,1024]{2,1,0:T(8,128)(2,1)} collective-permute-done((bf16[2,512,1024]{2,1,0:T(8,128)(2,1)}, bf16[2,512,1024]{2,1,0:T(8,128)(2,1)}, u32[]{:S(2)}, u32[]{:S(2)}) %collective-permute-start.2) | collective-permute-done | bytes 2097184 | tf_op jit(solution)/shard_map/ppermute | solution.py:19
  151.7 22.2 %hop_step.3 = (bf16[512,1024]{1,0:T(8,128)(2,1)S(1)}, f32[512,1024]{1,0:T(8,128)S(1)}, f32[512,1024]{1,0:T(8,128)S(1)}, f32[512,1024]{1,0:T(8,128)S(1)}, bf16[2,512,1024]{2,1,0:T(8,128)(2,1)S(1)}) custom-call(f32[16]{0:T(128)S(1)} %multiply_power_fusion.slopes, s32[512,1]{1,0:T(8,128)S(1)} %copy.19.seg_col, s32[1,512]{1,0:T(1,128)S(1)} %broadcast_select_fusion.seg_row, ...), custom_call_target="tpu_custom_call" | custom-call | flops 12582912 | bytes 524288 | tf_op jit(solution)/shard_map/hop_step/pallas_call | solution.py:213
  173.9 2.4 convolution_convert_fusion
  177.2 1.5 dynamic-slice_bitcast_fusion
  178.7 1.1 copy-done.28
  179.8 3.0 fusion.1
  182.9 1.2 constant_dynamic-slice_fusion.1
  184.1 1.5 collective-permute-start.4
  185.6 2.2 fusion
  187.8 1.3 copy-done.32
  189.1 1.0 constant_dynamic-slice_fusion
  190.2 0.5 collective-permute-start.7
  190.7 1.5 collective-permute-start.9
  192.2 1.6 copy-done.6
  193.8 1.6 copy-done.8
  195.4 1.6 copy-done.10
  197.0 1.6 copy-done.18
  198.6 1.6 copy-done.20
  200.2 11.8 %own_backward.3 = (bf16[512,1024]{1,0:T(8,128)(2,1)S(1)}, f32[2,512,1024]{2,1,0:T(8,128)}) custom-call(f32[16]{0:T(128)S(1)} %multiply_power_fusion.slopes, s32[512,1]{1,0:T(8,128)S(1)} %copy.19.seg_col, s32[1,512]{1,0:T(1,128)S(1)} %copy-done.24, bf16[512,2048]{1,0:T(8,128)(2,1)S(1)} %bitcast.85, bf16[512,2048]{1,0:T(8,128)(2,1)S(1)} %bitcast.89, ...), custom_call_target="tpu_custom_call" | custom-call | flops 10485760 | bytes 524288 | tf_op jit(solution)/shard_map/own_backward/pallas_call | solution.py:245
  212.0 11.8 %own_backward.2 = (bf16[512,1024]{1,0:T(8,128)(2,1)S(1)}, f32[2,512,1024]{2,1,0:T(8,128)}) custom-call(f32[16]{0:T(128)S(1)} %multiply_power_fusion.slopes, s32[512,1]{1,0:T(8,128)S(1)} %copy.19.seg_col, s32[1,512]{1,0:T(1,128)S(1)} %copy-done.24, bf16[512,2048]{1,0:T(8,128)(2,1)S(1)} %bitcast.86, bf16[512,2048]{1,0:T(8,128)(2,1)S(1)} %bitcast.90, ...), custom_call_target="tpu_custom_call" | custom-call | flops 10485760 | bytes 524288 | tf_op jit(solution)/shard_map/own_backward/pallas_call | solution.py:245
  223.8 1.9 fusion.6
  225.8 6.7 %collective-permute-done.7 = bf16[1,1024,512]{2,1,0:T(8,128)(2,1)} collective-permute-done((bf16[1,1024,512]{2,1,0:T(8,128)(2,1)}, bf16[1,1024,512]{2,1,0:T(8,128)(2,1)}, u32[]{:S(2)}, u32[]{:S(2)}) %collective-permute-start.7) | collective-permute-done | bytes 1048608 | tf_op jit(solution)/shard_map/ppermute | solution.py:32
  232.4 1.5 fusion.7
  234.1 1.1 dynamic-slice_bitcast_fusion.2
  235.2 1.6 collective-permute-start.8
  236.8 28.1 %collective-permute-done.8 = bf16[2,2,256,512]{3,2,1,0:T(8,128)(2,1)} collective-permute-done((bf16[2,2,256,512]{3,2,1,0:T(8,128)(2,1)}, bf16[2,2,256,512]{3,2,1,0:T(8,128)(2,1)}, u32[]{:S(2)}, u32[]{:S(2)}) %collective-permute-start.8) | collective-permute-done | bytes 1048608 | tf_op jit(solution)/shard_map/ppermute | solution.py:32
  265.0 1.8 fusion.2
  266.8 0.8 dynamic-slice_bitcast_fusion.3
  267.7 2.6 collective-permute-start.10
  270.3 1.5 maximum_bitcast_fusion
  271.8 20.5 %collective-permute-done.10 = bf16[2,256,512]{2,1,0:T(8,128)(2,1)} collective-permute-done((bf16[2,256,512]{2,1,0:T(8,128)(2,1)}, bf16[2,256,512]{2,1,0:T(8,128)(2,1)}, u32[]{:S(2)}, u32[]{:S(2)}) %collective-permute-start.10) | collective-permute-done | bytes 524320 | tf_op jit(solution)/shard_map/ppermute | solution.py:32
  292.2 1.2 fusion.8
  293.5 2.5 add_convert_fusion.1
  296.0 5.7 %collective-permute-done.11 = bf16[256,512]{1,0:T(8,128)(2,1)S(1)} collective-permute-done((bf16[256,512]{1,0:T(8,128)(2,1)S(1)}, bf16[256,512]{1,0:T(8,128)(2,1)S(1)}, u32[]{:S(2)}, u32[]{:S(2)}) %collective-permute-start.11) | collective-permute-done | bytes 262176 | tf_op jit(solution)/shard_map/ppermute | solution.py:32
  301.7 0.8 fusion.9
  302.7 2.0 copy-done.35
  304.7 2.5 add_convert_fusion
  307.4 1.5 maximum_bitcast_fusion.1
  309.0 1.5 maximum_bitcast_fusion.2
  310.5 5.9 %all-gather.2.cloned.1.call-done = bf16[256,2048]{1,0:T(8,128)(2,1)} async-done(((bf16[256,512]{1,0:T(8,128)(2,1)}), bf16[256,2048]{1,0:T(8,128)(2,1)}) %all-gather.2.cloned.1.call-update) | async-done | bytes 1048592 | tf_op jit(solution)/shard_map/all_gather | solution.py:259
  316.4 2.3 copy.33
  (81 shorter events, 1.8 us)
Async XLA Ops:
  7.2 19.1 %copy-start = (bf16[1,512,2048]{2,1,0:T(8,128)(2,1)S(1)}, bf16[1,512,2048]{2,1,0:T(8,128)(2,1)}, u32[]{:S(2)}) copy-start(bf16[1,512,2048]{2,1,0:T(8,128)(2,1)} %param.9) | copy-start | bytes 6291460
  7.2 309.2 %all-gather.2.cloned.1.call-start = ((), (), s32[]{:S(2)}) async-start(), calls=%async_computation | async-start | bytes 1310720 | tf_op jit(solution)/shard_map/all_gather | solution.py:259
  7.2 19.1 %slice-start = ((s8[8388608]{0:T(1024)(128)(4,1)}), s8[4194304]{0:T(1024)(128)(4,1)S(1)}, s32[]{:S(2)}) async-start(s8[8388608]{0:T(1024)(128)(4,1)} %bitcast.104), calls=%async_computation.1 | async-start | bytes 8388608
  10.0 7.9 %copy-start.24 = (s32[1,512]{1,0:T(1,128)S(1)}, s32[1,512]{1,0:T(1,128)}, u32[]{:S(2)}) copy-start(s32[1,512]{1,0:T(1,128)} %seg_row.5) | copy-start | bytes 6148
  10.0 16.3 %slice-start.1 = ((s8[8388608]{0:T(1024)(128)(4,1)}), s8[4194304]{0:T(1024)(128)(4,1)S(1)}, s32[]{:S(2)}) async-start(s8[8388608]{0:T(1024)(128)(4,1)} %bitcast.104), calls=%async_computation.2 | async-start | bytes 8388608
  11.6 51.3 %collective-permute-start.1 = (bf16[2,512,1024]{2,1,0:T(8,128)(2,1)}, bf16[2,512,1024]{2,1,0:T(8,128)(2,1)}, u32[]{:S(2)}, u32[]{:S(2)}) collective-permute-start(bf16[2,512,1024]{2,1,0:T(8,128)(2,1)} %pad_maximum_fusion), channel_id=1, source_target_pairs={{0,4},{4,8},{8,12},{12,16},{16,20},{20,24},{24,28},{1,5},{5,9},{9,... | collective-permute-start | bytes 6291464 | tf_op jit(solution)/shard_map/ppermute | solution.py:19
  17.9 45.0 %collective-permute-start = (s32[1,512]{1,0:T(1,128)S(1)}, s32[1,512]{1,0:T(1,128)S(1)}, u32[]{:S(2)}, u32[]{:S(2)}) collective-permute-start(s32[1,512]{1,0:T(1,128)S(1)} %copy-done.24), channel_id=1, source_target_pairs={{0,4},{4,8},{8,12},{12,16},{16,20},{20,24},{24,28},{1,5},{5,9},{9,... | collective-permute-start | bytes 6152 | tf_op jit(solution)/shard_map/ppermute | solution.py:19
  21.5 130.2 %collective-permute-start.2 = (bf16[2,512,1024]{2,1,0:T(8,128)(2,1)}, bf16[2,512,1024]{2,1,0:T(8,128)(2,1)}, u32[]{:S(2)}, u32[]{:S(2)}) collective-permute-start(bf16[2,512,1024]{2,1,0:T(8,128)(2,1)} %pad_maximum_fusion.1), channel_id=1, source_target_pairs={{0,4},{4,8},{8,12},{12,16},{16,20},{20,24},{24,28},{1,5},{5,9},{9,... | collective-permute-start | bytes 6291464 | tf_op jit(solution)/shard_map/ppermute | solution.py:19
  32.5 1.6 copy-start.2
  34.1 1.6 copy-start.7
  35.7 1.6 copy-start.9
  37.3 25.7 %copy-start.3 = (bf16[1,512,2048]{2,1,0:T(8,128)(2,1)S(1)}, bf16[1,512,2048]{2,1,0:T(8,128)(2,1)}, u32[]{:S(2)}) copy-start(bf16[1,512,2048]{2,1,0:T(8,128)(2,1)} %param.6) | copy-start | bytes 6291460
  55.1 2.1 copy-start.11
  85.2 1.4 copy-start.12
  86.5 1.4 copy-start.14
  87.9 1.3 copy-start.16
  89.2 1.0 copy-start.26
  90.2 83.7 %collective-permute-start.5 = (bf16[2,512,1024]{2,1,0:T(8,128)(2,1)}, bf16[2,512,1024]{2,1,0:T(8,128)(2,1)}, u32[]{:S(2)}, u32[]{:S(2)}) collective-permute-start(bf16[2,512,1024]{2,1,0:T(8,128)(2,1)} %get-tuple-element.40), channel_id=1, source_target_pairs={{4,0},{8,4},{12,8},{16,12},{20,16},{24,20},{28,24},{5,1},{9,5},{13... | collective-permute-start | bytes 6291464 | tf_op jit(solution)/shard_map/ppermute | solution.py:19
  95.7 2.8 copy-start.27
  95.7 56.0 %copy-start.4 = (bf16[1,512,2048]{2,1,0:T(8,128)(2,1)S(1)}, bf16[1,512,2048]{2,1,0:T(8,128)(2,1)}, u32[]{:S(2)}) copy-start(bf16[1,512,2048]{2,1,0:T(8,128)(2,1)} %param.6) | copy-start | bytes 6291460
  98.5 81.4 %collective-permute-start.3 = (bf16[2,1024,512]{2,1,0:T(8,128)(2,1)}, bf16[2,1024,512]{2,1,0:T(8,128)(2,1)}, u32[]{:S(2)}, u32[]{:S(2)}) collective-permute-start(bf16[2,1024,512]{2,1,0:T(8,128)(2,1)} %dynamic-slice_bitcast_fusion.1), channel_id=1, source_target_pairs={{0,1},{1,0},{2,3},{3,2},{4,5},{5,4},{6,7},{7,6},{8,9},{9,8},{10,11... | collective-permute-start | bytes 6291464 | tf_op jit(solution)/shard_map/ppermute | solution.py:32
  173.9 2.4 copy-start.17
  173.9 2.4 copy-start.19
  173.9 2.7 copy-start.21
  173.9 3.3 %copy-start.25 = (bf16[2,512,1024]{2,1,0:T(8,128)(2,1)}, bf16[2,512,1024]{2,1,0:T(8,128)(2,1)S(1)}, u32[]{:S(2)}) copy-start(bf16[2,512,1024]{2,1,0:T(8,128)(2,1)S(1)} %get-tuple-element.49) | copy-start | bytes 6291460
  177.2 2.6 copy-start.28
  179.8 5.8 %collective-permute-start.6 = (bf16[2,1024,512]{2,1,0:T(8,128)(2,1)}, bf16[2,1024,512]{2,1,0:T(8,128)(2,1)}, u32[]{:S(2)}, u32[]{:S(2)}) collective-permute-start(bf16[2,1024,512]{2,1,0:T(8,128)(2,1)} %dynamic-slice_bitcast_fusion), channel_id=1, source_target_pairs={{0,1},{1,0},{2,3},{3,2},{4,5},{5,4},{6,7},{7,6},{8,9},{9,8},{10,11... | collective-permute-start | bytes 6291464 | tf_op jit(solution)/shard_map/ppermute | solution.py:32
  179.8 5.8 %copy-start.29 = (bf16[128,4,8,512]{3,2,0,1:T(8,128)(2,1)S(1)}, bf16[128,4,8,512]{3,2,0,1:T(8,128)(2,1)}, u32[]{:S(2)}) copy-start(bf16[128,4,8,512]{3,2,0,1:T(8,128)(2,1)} %copy-done.28) | copy-start | bytes 12582916
  182.8 2.7 copy-start.30
  184.1 39.7 %collective-permute-start.4 = (bf16[1,1024,512]{2,1,0:T(8,128)(2,1)}, bf16[1,1024,512]{2,1,0:T(8,128)(2,1)}, u32[]{:S(2)}, u32[]{:S(2)}) collective-permute-start(bf16[1,1024,512]{2,1,0:T(8,128)(2,1)} %constant_dynamic-slice_fusion.1), channel_id=1, source_target_pairs={{0,2},{1,3},{2,0},{3,1},{4,6},{5,7},{6,4},{7,5},{8,10},{9,11},{10,... | collective-permute-start | bytes 3145736 | tf_op jit(solution)/shard_map/ppermute | solution.py:32
  187.8 1.3 copy-start.32
  189.1 3.1 copy-start.5
  190.2 42.3 %collective-permute-start.7 = (bf16[1,1024,512]{2,1,0:T(8,128)(2,1)}, bf16[1,1024,512]{2,1,0:T(8,128)(2,1)}, u32[]{:S(2)}, u32[]{:S(2)}) collective-permute-start(bf16[1,1024,512]{2,1,0:T(8,128)(2,1)} %constant_dynamic-slice_fusion), channel_id=1, source_target_pairs={{0,2},{1,3},{2,0},{3,1},{4,6},{5,7},{6,4},{7,5},{8,10},{9,11},{10,... | collective-permute-start | bytes 3145736 | tf_op jit(solution)/shard_map/ppermute | solution.py:32
  190.7 76.1 %collective-permute-start.9 = (bf16[2,512,1024]{2,1,0:T(8,128)(2,1)}, bf16[2,512,1024]{2,1,0:T(8,128)(2,1)}, u32[]{:S(2)}, u32[]{:S(2)}) collective-permute-start(bf16[2,512,1024]{2,1,0:T(8,128)(2,1)} %copy-done.25), channel_id=1, source_target_pairs={{4,0},{8,4},{12,8},{16,12},{20,16},{24,20},{28,24},{5,1},{9,5},{13... | collective-permute-start | bytes 6291464 | tf_op jit(solution)/shard_map/ppermute | solution.py:19
  192.2 1.6 copy-start.6
  193.8 1.6 copy-start.8
  195.4 1.6 copy-start.10
  197.0 1.6 copy-start.18
  198.6 1.6 copy-start.20
  200.2 11.8 %copy-start.13 = (f32[512,1024]{1,0:T(8,128)S(1)}, f32[512,1024]{1,0:T(8,128)}, u32[]{:S(2)}) copy-start(f32[512,1024]{1,0:T(8,128)} %copy-done.12) | copy-start | bytes 6291460
  200.2 11.8 %copy-start.15 = (f32[512,1024]{1,0:T(8,128)S(1)}, f32[512,1024]{1,0:T(8,128)}, u32[]{:S(2)}) copy-start(f32[512,1024]{1,0:T(8,128)} %copy-done.14) | copy-start | bytes 6291460
  212.0 11.8 %copy-start.31 = (bf16[2,1024,512]{2,1,0:T(8,128)(2,1)S(1)}, bf16[2,1024,512]{2,1,0:T(8,128)(2,1)}, u32[]{:S(2)}) copy-start(bf16[2,1024,512]{2,1,0:T(8,128)(2,1)} %copy-done.30) | copy-start | bytes 6291460
  223.8 10.1 %copy-start.22 = (bf16[512,1024]{1,0:T(8,128)(2,1)}, bf16[512,1024]{1,0:T(8,128)(2,1)S(1)}, u32[]{:S(2)}) copy-start(bf16[512,1024]{1,0:T(8,128)(2,1)S(1)} %get-tuple-element.33) | copy-start | bytes 3145732
  223.8 8.6 %copy-start.33 = (bf16[2,1024,512]{2,1,0:T(8,128)(2,1)S(1)}, bf16[2,1024,512]{2,1,0:T(8,128)(2,1)}, u32[]{:S(2)}) copy-start(bf16[2,1024,512]{2,1,0:T(8,128)(2,1)} %copy-done.32) | copy-start | bytes 6291460
  234.1 2.7 copy-start.34
  235.2 29.7 %collective-permute-start.8 = (bf16[2,2,256,512]{3,2,1,0:T(8,128)(2,1)}, bf16[2,2,256,512]{3,2,1,0:T(8,128)(2,1)}, u32[]{:S(2)}, u32[]{:S(2)}) collective-permute-start(bf16[2,2,256,512]{3,2,1,0:T(8,128)(2,1)} %dynamic-slice_bitcast_fusion.2), channel_id=1, source_target_pairs={{0,8},{4,12},{8,0},{12,4},{16,24},{20,28},{24,16},{28,20},{1,9},{5... | collective-permute-start | bytes 3145736 | tf_op jit(solution)/shard_map/ppermute | solution.py:32
  236.8 33.4 %copy-start.23 = (bf16[512,1024]{1,0:T(8,128)(2,1)S(1)}, bf16[512,1024]{1,0:T(8,128)(2,1)}, u32[]{:S(2)}) copy-start(bf16[512,1024]{1,0:T(8,128)(2,1)} %copy-done.22) | copy-start | bytes 3145732
  267.7 24.6 %collective-permute-start.10 = (bf16[2,256,512]{2,1,0:T(8,128)(2,1)}, bf16[2,256,512]{2,1,0:T(8,128)(2,1)}, u32[]{:S(2)}, u32[]{:S(2)}) collective-permute-start(bf16[2,256,512]{2,1,0:T(8,128)(2,1)} %dynamic-slice_bitcast_fusion.3), channel_id=1, source_target_pairs={{0,16},{4,20},{8,24},{12,28},{16,0},{20,4},{24,8},{28,12},{1,17},{... | collective-permute-start | bytes 1572872 | tf_op jit(solution)/shard_map/ppermute | solution.py:32
  270.3 23.3 %copy-start.36 = (f32[2,512,1024]{2,1,0:T(8,128)S(1)}, f32[2,512,1024]{2,1,0:T(8,128)}, u32[]{:S(2)}) copy-start(f32[2,512,1024]{2,1,0:T(8,128)} %get-tuple-element.44) | copy-start | bytes 12582916
  293.5 8.3 %collective-permute-start.11 = (bf16[256,512]{1,0:T(8,128)(2,1)S(1)}, bf16[256,512]{1,0:T(8,128)(2,1)S(1)}, u32[]{:S(2)}, u32[]{:S(2)}) collective-permute-start(bf16[256,512]{1,0:T(8,128)(2,1)S(1)} %dynamic-slice_bitcast_fusion.4), channel_id=1, source_target_pairs={{0,4},{4,0},{8,12},{12,8},{16,20},{20,16},{24,28},{28,24},{1,5},{5... | collective-permute-start | bytes 786440 | tf_op jit(solution)/shard_map/ppermute | solution.py:32
  302.5 2.2 copy-start.35
  308.9 9.7 %copy-start.1 = (bf16[1,512,2048]{2,1,0:T(8,128)(2,1)S(1)}, bf16[1,512,2048]{2,1,0:T(8,128)(2,1)}, u32[]{:S(2)}) copy-start(bf16[1,512,2048]{2,1,0:T(8,128)(2,1)} %param.9) | copy-start | bytes 6291460
Sparse Core Ops, SparseCore 0:
  302.7 13.6 all-gather.1
